TPU v7x, 32 devices: a whole 2x2x4 slice. The times are simulated.
32 devices in a mesh: dp: 8 (over y, x, core), batch: 4 (over z).
Axes of the slice: x: 2, y: 2, z: 4, core: 2. Of those that a mesh axis runs over, the one named last changes fastest.
Arguments:
- activations_in: float32 [32, 1024, 512], P(('dp', 'batch')), may hold values from -6 to 6
- gains: float32 [2, 2, 512], replicated, may hold values from 0.5 to 1.5
- shifts: float32 [2, 2, 512], replicated, may hold values from -2.5 to 2.5
- qkv_weights: bfloat16 [2, 3, 512, 512], replicated, may hold values from -0.25 to 0.25
- out_weights: bfloat16 [2, 512, 512], replicated, may hold values from -2 to 2
- up_weights: bfloat16 [2, 512, 2048], replicated, may hold values from -0.25 to 0.25
- up_bias: float32 [2, 2048], replicated, may hold values from -2.5 to 2.5
- down_weights: bfloat16 [2, 2048, 512], replicated, may hold values from -0.125 to 0.125
- down_bias: float32 [2, 512], replicated, may hold values from -2.5 to 2.5
- feature_maps: float32 [2, 8, 64, 256], replicated, may hold values from -4 to 4
- lengths: int32 [32, 6], P(('dp', 'batch')), may hold values from 18 to 146, as said below
- cotangent: float32 [32, 1024, 512], P(('dp', 'batch')), may hold values from -6 to 6
Outputs:
- activations_out: float32 [32, 1024, 512], P(('dp', 'batch'))
- input_grad: float32 [32, 1024, 512], P(('dp', 'batch'))
- gains_grad: float32 [2, 2, 512], P(None, None, 'batch')
- shifts_grad: float32 [2, 2, 512], P(None, None, 'batch')
- qkv_grad: float32 [2, 3, 512, 512], P(None, None, None, 'batch')
- out_grad: float32 [2, 512, 512], P(None, None, 'batch')
- up_grad: float32 [2, 512, 2048], P(None, None, 'batch')
- up_bias_grad: float32 [2, 2048], P(None, 'batch')
- down_grad: float32 [2, 2048, 512], P(None, None, 'batch')
- down_bias_grad: float32 [2, 512], P(None, 'batch')
Inputs may be any that keep to these rules, and one draw needn't show every extreme that they name: `lengths`: each of a row's 6 proteins has 18 to 146 tokens; in every row one protein has exactly 146 and another exactly 18; the remaining positions of the row are padding.
All inputs are finite; a program needn't handle non-finite values.
Results may differ from a plain program's by a relative error of at most 0.015.
The roundings to bfloat16 on the way count: a program that leaves them out, or rounds other values in their place, can miss the bound.
Values sent between devices are 32-bit elements; how exact they have to be, the bound alone decides.
No kernel may reach another device: no remote copies, remote signals or barrier semaphores. Data moves between devices by JAX's collectives and lax.ppermute only.
A program may use at most 384 MiB of HBM per device.

v0:
```python
import functools
import math

import jax
import jax.numpy as jnp
from jax import lax
from jax.experimental import pallas as pl
from jax.experimental.pallas import tpu as pltpu
from jax.sharding import PartitionSpec as P

BLOCK = 256
BLOCKS = 3
LIVE = BLOCK * BLOCKS
REACH = 160
LANES = 128
NDOC = 6
MIB = 1 << 20
F32 = jnp.float32
BF16 = jnp.bfloat16
LOG2E = 1.4426950408889634
NT = (((1,), (1,)), ((), ()))


def dot(a, b):
    return jnp.dot(a, b, preferred_element_type=F32)


def dot_nt(a, b):
    return lax.dot_general(a, b, NT, preferred_element_type=F32)


def params_for(mib):
    return pltpu.CompilerParams(vmem_limit_bytes=mib * MIB)


def call(body, after, *, grid, in_specs, out_specs, out_shape, prefetch, operands, scratch=(), aliases=(), mib=63, us=3.0, name):
    scalars, count = len(prefetch), len(after)

    def ordered(*refs):
        body(*refs[:scalars], *refs[scalars + count :])

    return pl.pallas_call(
        ordered,
        grid_spec=pltpu.PrefetchScalarGridSpec(
            num_scalar_prefetch=scalars,
            grid=grid,
            in_specs=[pl.BlockSpec(memory_space=pl.ANY)] * count + list(in_specs),
            out_specs=out_specs,
            scratch_shapes=list(scratch),
        ),
        out_shape=out_shape,
        input_output_aliases={scalars + count + operand: output for operand, output in aliases},
        compiler_params=params_for(mib),
        cost_estimate=pl.CostEstimate(flops=int(us * 1.15e9), bytes_accessed=0, transcendentals=0),
        name=name,
    )(*prefetch, *after, *operands)


def constant(*shape):
    return pl.BlockSpec(shape, lambda *_: (0,) * len(shape), pipeline_mode=pl.Buffered(1))


def resident(*shape):
    return pl.BlockSpec(shape, lambda *_: (0,) * len(shape))


def of_layer(layer, array):
    return pl.BlockSpec((None,) + array.shape[1:], lambda *_: (layer,) + (0,) * (array.ndim - 1), pipeline_mode=pl.Buffered(1))


def anywhere():
    return pl.BlockSpec(memory_space=pl.ANY)


def fetch(step, begin, end, sources, targets, sems):
    copies = [pltpu.make_async_copy(source, target, sems.at[k]) for k, (source, target) in enumerate(zip(sources, targets))]

    @pl.when(step == begin)
    def _():
        for copy in copies:
            copy.start()

    @pl.when(step == end)
    def _():
        for copy in copies:
            copy.wait()


def normalize(values):
    centered = values - jnp.mean(values, axis=-1, keepdims=True)
    rstd = lax.rsqrt(jnp.mean(centered * centered, axis=-1, keepdims=True) + 1e-05)
    return centered * rstd, rstd


def norm_pull(grad, gain, unit, rstd):
    p = grad * gain
    return rstd * (p - jnp.mean(p, axis=-1, keepdims=True) - unit * jnp.mean(p * unit, axis=-1, keepdims=True))


def split_two(values):
    high = values.astype(BF16)
    return high, (values - high.astype(F32)).astype(BF16)


def protein_ids(len_ref, position):
    bound = jnp.int32(0)
    ids = jnp.zeros(position.shape, jnp.int32)
    for j in range(NDOC):
        bound = bound + len_ref[j]
        ids = ids + (position >= bound).astype(jnp.int32)
    return ids


def token_count(len_ref):
    total = jnp.int32(0)
    for j in range(NDOC):
        total = total + len_ref[j]
    return total


def pair_mask(len_ref, shape, first_row, first_col, causal_rows):
    rows = lax.broadcasted_iota(jnp.int32, shape, 0) + first_row
    cols = lax.broadcasted_iota(jnp.int32, shape, 1) + first_col
    same = protein_ids(len_ref, rows) == protein_ids(len_ref, cols)
    ordered = (rows >= cols) if causal_rows else (cols >= rows)
    return jnp.where(same & ordered, 1.0, 0.0).astype(BF16)


def fill_masks(len_ref, own_ref, before_ref, causal_rows):
    for b in range(BLOCKS):
        own_ref[b] = pair_mask(len_ref, (BLOCK, BLOCK), b * BLOCK, b * BLOCK, causal_rows)
    for b in range(1, BLOCKS):
        if causal_rows:
            before_ref[b - 1] = pair_mask(len_ref, (REACH, BLOCK), b * BLOCK, (b - 1) * BLOCK, True)
        else:
            before_ref[b - 1] = pair_mask(len_ref, (REACH, BLOCK), b * BLOCK - REACH, b * BLOCK, False)


def attn_fwd_body(layer, step, low_ref, low_t_ref, len_ref, x_ref, gain_ref, shift_ref, w_ref, fm_ref, normed_t_ref, phi_q_ref, phi_k_ref, uq_ref, uk_ref,
                  v_ref, att_ref, rden_ref, normed_ref, proj_ref, own_ref, before_ref, num_ref):
    columns_here = pl.ds(pl.multiple_of(step * LANES, LANES), LANES)

    @pl.when(step == 0)
    def _():
        fill_masks(len_ref, own_ref, before_ref, True)
        for b in range(BLOCKS):
            rows = pl.ds(b * BLOCK, BLOCK)
            unit, _ = normalize(x_ref[rows, :])
            normed = (unit * gain_ref[layer, 0:1, :] + shift_ref[layer, 0:1, :]).astype(BF16)
            normed_ref[rows, :] = normed
            normed_t_ref[:, rows] = normed.T
        for j in range(3):
            for half in range(2):
                got = dot(normed_ref[...], w_ref[j, :, half * 256 : half * 256 + 256])
                proj_ref[j, 2 * half] = got[:, :LANES]
                proj_ref[j, 2 * half + 1] = got[:, LANES:]

    lane = lax.broadcasted_iota(jnp.int32, (BLOCK, LANES), 1) < 64
    uq_ref[0] = proj_ref[0, step]
    uk_ref[0] = proj_ref[1, step]
    v_ref[0] = proj_ref[2, step].astype(BF16)
    first_head = lax.broadcasted_iota(jnp.int32, (LANES, 256), 0) < 64
    minus = [jnp.where(first_head, -1.0, 0.0).astype(BF16), jnp.where(first_head, 0.0, -1.0).astype(BF16)]
    stacked = []
    for head in range(2):
        high, low = split_two(fm_ref[head] * (64.0 ** (-0.25) * LOG2E))
        stacked.append(jnp.concatenate([high, low, high, low, minus[head], minus[head]], axis=0))
    for which, phi_ref in ((0, phi_q_ref), (1, phi_k_ref)):
        for b in range(BLOCKS):
            rows = pl.ds(b * BLOCK, BLOCK)
            u = proj_ref[which, step, rows, :]
            turned = pltpu.roll(u, 64, 1)
            squares = split_two(u * u * (LOG2E / 16.0) + 0.0625)
            for head in range(2):
                twice = jnp.where(lane, u, turned) if head == 0 else jnp.where(lane, turned, u)
                exponent = dot(jnp.concatenate(split_two(twice) + squares, axis=1), stacked[head])
                phi_ref[head, rows, :] = jnp.exp2(exponent).astype(BF16)
    ones = jnp.ones((BLOCK, LANES), BF16)
    for b in range(BLOCKS):
        rows = pl.ds(b * BLOCK, BLOCK)
        v_now = jnp.concatenate([v_ref[0, rows, :], ones], axis=1)
        for head in range(2):
            weights = dot_nt(phi_q_ref[head, rows, :], phi_k_ref[head, rows, :]).astype(BF16) * own_ref[b]
            num_ref[head] = dot(weights, v_now)
            if b > 0:
                earlier = pl.ds((b - 1) * BLOCK, BLOCK)
                v_before = jnp.concatenate([v_ref[0, earlier, :], ones], axis=1)
                weights = dot_nt(phi_q_ref[head, pl.ds(b * BLOCK, REACH), :], phi_k_ref[head, earlier, :])
                num_ref[head, :REACH, :] += dot(weights.astype(BF16) * before_ref[b - 1], v_before)
        rden = 1.0 / jnp.where(lane, num_ref[0, :, LANES:], num_ref[1, :, LANES:])
        attended = jnp.where(lane, num_ref[0, :, :LANES], num_ref[1, :, :LANES]) * rden
        position = lax.broadcasted_iota(jnp.int32, (BLOCK, LANES), 0) + b * BLOCK
        attended = jnp.where(position < token_count(len_ref), attended, 0.0)
        rden_ref[0, rows, :] = rden
        att_ref[0, rows, :] = attended
        low = attended.astype(BF16)
        low_ref[rows, columns_here] = low
        low_t_ref[columns_here, rows] = low.T


def gelu_terms(pre):
    lifted = 0.5 + 0.5 * lax.erf(pre * math.sqrt(0.5))
    return pre * lifted, lifted + pre * (jnp.exp2(pre * pre * (-0.5 * LOG2E)) * (1.0 / math.sqrt(2.0 * math.pi)))


def ff_fwd_body(layer, step, x_ref, low_ref, wo_ref, gain_ref, shift_ref, up_ref, up_bias_ref, down_ref, down_bias_ref, out_ref, mid_ref):
    mid_ref[...] = x_ref[...]

    @pl.when(step < BLOCKS)
    def _():
        mid_ref[...] += dot(low_ref[...], wo_ref[...])

    mid = mid_ref[...]
    unit, _ = normalize(mid)
    normed = (unit * gain_ref[layer, 1:2, :] + shift_ref[layer, 1:2, :]).astype(BF16)
    total = mid + down_bias_ref[layer : layer + 1, :]
    for first in range(0, up_ref.shape[1], 512):
        cols = slice(first, first + 512)
        pre = dot(normed, up_ref[:, cols]) + up_bias_ref[layer : layer + 1, cols]
        act = (pre * (0.5 + 0.5 * lax.erf(pre * math.sqrt(0.5)))).astype(BF16)
        total = total + dot(act, down_ref[cols, :])
    out_ref[...] = total


def attn_bwd_body(len_ref, att_g_ref, att_ref, rden_ref, phi_q_ref, phi_k_ref, uq_ref, uk_ref, v_ref, fm_ref,
                  dq_ref, dk_ref, dv_ref, own_ref, before_ref, own_t_ref, before_t_ref,
                  x_ref, y_ref, dn_ref, d_phi_q, d_phi_k, d_v, raw_ref):
    step = pl.program_id(0)

    @pl.when(step == 0)
    def _():
        fill_masks(len_ref, own_ref, before_ref, True)
        fill_masks(len_ref, own_t_ref, before_t_ref, False)

    lane = lax.broadcasted_iota(jnp.int32, (BLOCK, LANES), 1) < 64
    one = jnp.ones((BLOCK, LANES), BF16)
    for b in range(BLOCKS):
        rows = pl.ds(b * BLOCK, BLOCK)
        position = lax.broadcasted_iota(jnp.int32, (BLOCK, LANES), 0) + b * BLOCK
        dn = jnp.where(position < token_count(len_ref), att_g_ref[rows, :] * rden_ref[0, rows, :], 0.0)
        turned = pltpu.roll(-(dn * att_ref[0, rows, :]), 64, 1)
        dn_ref[rows, :] = dn.astype(BF16)
        v_low = v_ref[0, rows, :]
        for head in range(2):
            first = lane if head == 0 else jnp.logical_not(lane)
            high, low = split_two(jnp.where(first, dn, turned))
            x_ref[head, rows, :] = jnp.concatenate([high, low], axis=1)
            y = jnp.where(first, v_low.astype(F32), 1.0).astype(BF16)
            y_ref[head, rows, :] = jnp.concatenate([y, y], axis=1)
    for head in range(2):
        for b in range(BLOCKS):
            rows = pl.ds(b * BLOCK, BLOCK)
            x, y = x_ref[head, rows, :], y_ref[head, rows, :]
            phi_q, phi_k = phi_q_ref[head, rows, :], phi_k_ref[head, rows, :]
            d_kernel = dot_nt(x, y).astype(BF16) * own_ref[b]
            d_phi_q[rows, :] = dot(d_kernel, phi_k)
            d_kernel_t = dot_nt(y, x).astype(BF16) * own_t_ref[b]
            d_phi_k[rows, :] = dot(d_kernel_t, phi_q)
            kernel_t = dot_nt(phi_k, phi_q).astype(BF16) * own_t_ref[b]
            d_v[head, rows, :] = dot(kernel_t, dn_ref[rows, :])
            if b > 0:
                earlier = pl.ds((b - 1) * BLOCK, BLOCK)
                top = pl.ds(b * BLOCK, REACH)
                bottom = pl.ds(b * BLOCK - REACH, REACH)
                d_kernel = dot_nt(x_ref[head, top, :], y_ref[head, earlier, :]).astype(BF16) * before_ref[b - 1]
                d_phi_q[top, :] += dot(d_kernel, phi_k_ref[head, earlier, :])
                d_kernel_t = dot_nt(y_ref[head, bottom, :], x).astype(BF16) * before_t_ref[b - 1]
                d_phi_k[bottom, :] += dot(d_kernel_t, phi_q)
                kernel_t = dot_nt(phi_k_ref[head, bottom, :], phi_q).astype(BF16) * before_t_ref[b - 1]
                d_v[head, bottom, :] += dot(kernel_t, dn_ref[rows, :])
        high, low = split_two(fm_ref[head])
        stacked = jnp.concatenate([high, low, jnp.ones((LANES, 256), BF16)], axis=0)
        for which, d_phi, phi_ref in ((0, d_phi_q, phi_q_ref), (1, d_phi_k, phi_k_ref)):
            for b in range(BLOCKS):
                rows = pl.ds(b * BLOCK, BLOCK)
                d_projected = (d_phi[rows, :] * phi_ref[head, rows, :].astype(F32)).astype(BF16)
                raw_ref[which, head, rows, :] = dot_nt(d_projected, stacked)
    for b in range(BLOCKS):
        rows = pl.ds(b * BLOCK, BLOCK)
        for which, u_ref, out_ref in ((0, uq_ref, dq_ref), (1, uk_ref, dk_ref)):
            parts = []
            for head in range(2):
                raw = raw_ref[which, head, rows, :LANES]
                parts.append(raw + pltpu.roll(raw, 64, 1))
            along = jnp.where(lane, parts[0], parts[1])
            total = jnp.where(lane, raw_ref[which, 0, rows, LANES:], raw_ref[which, 1, rows, LANES:])
            grad = along * (64.0 ** (-0.25)) - u_ref[0, rows, :] * total * 0.125
            out_ref[rows, :] = grad.astype(BF16)
        dv_ref[rows, :] = jnp.where(lane, d_v[0, rows, :], d_v[1, rows, :]).astype(BF16)


def attn_bwd(layer, lengths, att_g, att, rden, phi_q, phi_k, uq, uk, v, fm, first, count, us, after=()):
    per_pair = pl.BlockSpec((1, LIVE, LANES), lambda p, *_: (first + p, 0, 0))
    per_head = pl.BlockSpec((2, LIVE, 256), lambda p, *_: (first + p, 0, 0))
    return call(
        attn_bwd_body,
        after,
        grid=(count,),
        prefetch=[lengths],
        operands=[att_g, att, rden, phi_q, phi_k, uq, uk, v, fm],
        in_specs=[pl.BlockSpec((LIVE, LANES), lambda p, *_: (0, first + p)), per_pair, per_pair, per_head, per_head, per_pair, per_pair, per_pair,
                  pl.BlockSpec((None, 2) + fm.shape[2:], lambda p, *_: (layer, first + p, 0, 0))],
        out_specs=[pl.BlockSpec((LIVE, LANES), lambda p, *_: (0, p))] * 3,
        scratch=[
            pltpu.VMEM((BLOCKS, BLOCK, BLOCK), BF16),
            pltpu.VMEM((BLOCKS - 1, REACH, BLOCK), BF16),
            pltpu.VMEM((BLOCKS, BLOCK, BLOCK), BF16),
            pltpu.VMEM((BLOCKS - 1, REACH, BLOCK), BF16),
            pltpu.VMEM((2, LIVE, 256), BF16),
            pltpu.VMEM((2, LIVE, 256), BF16),
            pltpu.VMEM((LIVE, LANES), BF16),
            pltpu.VMEM((LIVE, 256), F32),
            pltpu.VMEM((LIVE, 256), F32),
            pltpu.VMEM((2, LIVE, LANES), F32),
            pltpu.VMEM((2, 2, LIVE, 256), F32),
        ],
        out_shape=[jax.ShapeDtypeStruct((LIVE, count * LANES), BF16)] * 3,
        us=us,
        name="attn_backward",
    )


GROUPS = 4


def put(out_ref, ids, values, quarter, base):
    me, here = ids
    count = out_ref.shape[0]
    rows = values.shape[0] // count
    for portion in range(count):
        out_ref[portion ^ me, quarter ^ here, base : base + rows, :] = values[portion * rows : portion * rows + rows]


def columns(values, which):
    return values[:, which * LANES : which * LANES + LANES]


def group_of_qkv(half, group, refs):
    normed_t_ref, lefts = refs[0], refs[1:]
    runs = len(lefts) // 3
    tall = normed_t_ref.shape[0] // 2
    height = 3 * tall // GROUPS
    parts = []
    first = group * height
    while first < (group + 1) * height:
        j, start = divmod(first, tall)
        rows = min(tall - start, (group + 1) * height - first)
        normed_t = normed_t_ref[pl.ds(pl.multiple_of(half * tall + start, 16), rows), :]
        parts.append(jnp.concatenate([dot(normed_t, lefts[3 * run + j][...]) for run in range(runs)], axis=1))
        first += rows
    return jnp.concatenate(parts, axis=0) if len(parts) > 1 else parts[0]


def ff_bwd_body(layer, top, runs, parts, step, id_ref, *refs):
    extra_refs, refs = refs[: 3 * runs + (runs > 0)], refs[3 * runs + (runs > 0) :]
    if top:
        (x_ref, low_ref, g_ref, low_t_ref, gain_ref, shift_ref, up_ref, up_bias_ref, down_ref, down_bias_ref, wo_ref,
         out_ref, mid_g_ref, att_g_ref, small_ref, up_bias_g_ref, kept_ref,
         act_ref, pre_ref, g_t_ref, normed_t_ref, mid_low_ref, mid_ref) = refs
    else:
        (mid_ref, g_ref, low_t_ref, gain_ref, shift_ref, up_ref, up_bias_ref, down_ref, wo_ref,
         mid_g_ref, att_g_ref, small_ref, up_bias_g_ref, sent_ref, kept_ref,
         act_ref, pre_ref, g_t_ref, normed_t_ref, mid_low_ref) = refs
    hidden = up_ref.shape[1]
    quarters = kept_ref.shape[1]
    length = g_t_ref.shape[1]
    tiles = length // BLOCK
    share = hidden // quarters

    @pl.when(step == 0)
    def _():
        small_ref[...] = jnp.zeros_like(small_ref)
        up_bias_g_ref[...] = jnp.zeros_like(up_bias_g_ref)

    @pl.when(step < tiles)
    def _():
        if top:
            mid_ref[...] = x_ref[...]

            @pl.when(step < BLOCKS)
            def _():
                mid_ref[...] += dot(low_ref[...], wo_ref[...])

        rows = pl.ds(pl.multiple_of(step * BLOCK, BLOCK), BLOCK)
        mid = mid_ref[...]
        unit, rstd = normalize(mid)
        normed = (unit * gain_ref[layer, 1:2, :] + shift_ref[layer, 1:2, :]).astype(BF16)
        normed_t_ref[:, rows] = normed.T
        grad = g_ref[...]
        g_low = grad.astype(BF16)
        g_t_ref[:, rows] = g_low.T
        if top:
            total = mid + down_bias_ref[layer : layer + 1, :]
        back = jnp.zeros(grad.shape, F32)
        for quarter in range(quarters):
            cols = slice(quarter * share, quarter * share + share)
            pre = dot(normed, up_ref[:, cols]) + up_bias_ref[layer : layer + 1, cols]
            act, slope = gelu_terms(pre)
            act = act.astype(BF16)
            per_half = quarters // 2
            act_ref[quarter // per_half, rows, (quarter % per_half) * share : (quarter % per_half) * share + share] = act
            if top:
                total = total + dot(act, down_ref[cols, :])
            pre_low = (dot_nt(g_low, down_ref[cols, :]) * slope).astype(BF16)
            for which in range(share // LANES):
                pre_ref[which, rows, quarter * LANES : quarter * LANES + LANES] = columns(pre_low, which)
            up_bias_g_ref[:, cols] += jnp.sum(pre_low.astype(F32), axis=0, keepdims=True)
            back = back + dot_nt(pre_low, up_ref[:, cols])
        if top:
            out_ref[...] = total
        mid_g = grad + norm_pull(back, gain_ref[layer, 1:2, :], unit, rstd)
        mid_g_ref[...] = mid_g
        mid_low = mid_g.astype(BF16)
        small_ref[0:1, :] += jnp.sum(back * unit, axis=0, keepdims=True)
        small_ref[1:2, :] += jnp.sum(back, axis=0, keepdims=True)
        small_ref[2:3, :] += jnp.sum(g_low.astype(F32), axis=0, keepdims=True)

        @pl.when(step < BLOCKS)
        def _():
            mid_low_ref[rows, :] = mid_low
            att_g_ref[...] = dot_nt(mid_low, wo_ref[...])

    count = kept_ref.shape[0]
    if top:
        ids = (0, 0)
        halves = ((tiles, 0, kept_ref), (tiles + GROUPS, 1, kept_ref))
    else:
        ids = (id_ref[0] & (count - 1), id_ref[1])
        own = id_ref[0] // (parts // 2)
        halves = ((tiles, own ^ 1, sent_ref), (tiles + GROUPS, own, kept_ref))
    for first, half, end_ref in halves:
        for group in range(GROUPS):

            @pl.when(step == first + group)
            def _(half=half, group=group, end_ref=end_ref):
                wide = act_ref.shape[2] // GROUPS
                down = dot(g_t_ref[...], act_ref[half, :, group * wide : group * wide + wide])
                height = normed_t_ref.shape[0] * (share // LANES // 2) // GROUPS
                per_tile = normed_t_ref.shape[0] // height
                part = group % per_tile
                up = dot(normed_t_ref[part * height : part * height + height, :], pre_ref[half * (share // LANES // 2) + group // per_tile])
                tall = low_t_ref.shape[0] // 2 // GROUPS
                low_rows = pl.ds(pl.multiple_of(half * (low_t_ref.shape[0] // 2) + group * tall, tall), tall)
                out = dot(low_t_ref[low_rows, :], mid_low_ref[...])
                if runs:
                    extra = group_of_qkv(half, group, extra_refs)
                for quarter in range(quarters):
                    rows = slice(quarter * LANES, quarter * LANES + LANES)
                    pieces = [
                        jnp.concatenate([columns(down[rows], which) for which in range(wide // LANES)], axis=0),
                        columns(up, quarter),
                        columns(out, quarter),
                    ]
                    if runs:
                        pieces.append(columns(extra, quarter))
                    base = 0
                    for piece in pieces:
                        put(end_ref, ids, piece, quarter, base)
                        base += piece.shape[0] // count


def piece_shapes(parts, quarters, width, hidden):
    rows = hidden // parts + width * (hidden // quarters // LANES) // parts + width // parts
    return (parts // 2, quarters, rows, LANES)


def lower_body(layer, runs, parts, id_ref, *refs):
    extra = 3 * runs + 1
    step = pl.program_id(0)
    *refs, sems = refs
    late = refs[len(refs) - extra - 1 :]
    refs = refs[: len(refs) - extra - 1]
    low_t = extra + 2
    fetch(step, 0, pl.num_programs(0) - 2 * GROUPS, list(refs[:extra]) + [refs[low_t]], late, sems)
    ff_bwd_body(layer, False, runs, parts, step, id_ref, *late[:extra], *refs[extra:low_t], late[extra], *refs[low_t + 1 :])


def ff_bwd(layer, ids, parts, quarters, grad, low_t, gains, shifts, up, up_bias, down, wo, mid, qkv, after=()):
    length, width = grad.shape
    hidden = up.shape[2]
    tiles = length // BLOCK
    portions = parts // 2
    group = portions // GROUPS
    rows = pl.BlockSpec((BLOCK, width), lambda i, ids: (jnp.minimum(i, tiles - 1), 0))
    live = pl.BlockSpec((BLOCK, width), lambda i, ids: (jnp.minimum(i, BLOCKS - 1), 0))
    extra = [qkv[0]] + [part for run in qkv[1] for part in run]
    end = piece_shapes(parts, quarters, width, hidden)
    end = end[:2] + (end[2] + 3 * width // parts, LANES)

    def end_spec(first):
        return pl.BlockSpec((group,) + end[1:], lambda i, ids: (jnp.clip(i - first, 0, GROUPS - 1) ^ ((ids[0] & (portions - 1)) // group), 0, 0, 0))

    return call(
        functools.partial(lower_body, layer, len(extra) // 3, parts),
        after,
        grid=(tiles + 2 * GROUPS,),
        prefetch=[ids],
        operands=extra + [mid, grad, low_t, gains, shifts, up, up_bias, down, wo],
        in_specs=[anywhere() for _ in extra]
        + [rows, rows, anywhere(), constant(*gains.shape), constant(*shifts.shape), of_layer(layer, up), constant(*up_bias.shape)]
        + [of_layer(layer, down), of_layer(layer, wo)],
        out_specs=[rows, live, resident(8, width), resident(1, hidden), end_spec(tiles), end_spec(tiles + GROUPS)],
        scratch=ff_bwd_scratch(length, width, hidden, quarters)
        + [pltpu.VMEM(array.shape, array.dtype) for array in extra + [low_t]]
        + [pltpu.SemaphoreType.DMA((len(extra) + 1,))],
        out_shape=[
            jax.ShapeDtypeStruct((length, width), F32),
            jax.ShapeDtypeStruct((LIVE, width), F32),
            jax.ShapeDtypeStruct((8, width), F32),
            jax.ShapeDtypeStruct((1, hidden), F32),
            jax.ShapeDtypeStruct(end, F32),
            jax.ShapeDtypeStruct(end, F32),
        ],
        us=18.0,
        name="ff_backward",
    )


def ff_bwd_scratch(length, width, hidden, quarters):
    return [
        pltpu.VMEM((2, length, hidden // 2), BF16),
        pltpu.VMEM((hidden // quarters // LANES, length, quarters * LANES), BF16),
        pltpu.VMEM((width, length), BF16),
        pltpu.VMEM((width, length), BF16),
        pltpu.VMEM((LIVE, width), BF16),
    ]


def layer_body(layer, top, pairs, parts, len_ref, id_ref, *refs):
    x_ref, gain_ref, shift_ref, w_ref, fm_ref, wo_ref, up_ref, up_bias_ref, down_ref, down_bias_ref = refs[:10]
    refs = refs[10:]
    *refs, wo_late, up_late, down_late, sems = refs
    step = pl.program_id(0)
    fetch(step, 0, pairs, [ref.at[layer] for ref in (wo_ref, up_ref, down_ref)], [wo_late, up_late, down_late], sems)
    wo_ref, up_ref, down_ref = wo_late, up_late, down_late
    refs = tuple(refs)
    if top:
        (g_ref, *outs) = refs[:9]
        out_ref, mid_g_ref, att_g_ref, small_ref, up_bias_g_ref, kept_ref, low_t_ref = refs[9:15] + refs[21:22]
        attn_scratch, low_ref = refs[15:20], refs[20]
        ff_scratch = refs[22:]
    else:
        outs = refs[:8]
        low_t_ref, out_ref, mid_ref = refs[8:11]
        attn_scratch, low_ref = refs[11:16], refs[16]

    @pl.when(step < pairs)
    def _():
        attn_fwd_body(layer, step, low_ref, low_t_ref, len_ref, x_ref, gain_ref, shift_ref, w_ref, fm_ref, *outs, *attn_scratch)

    @pl.when(step >= pairs)
    def _():
        tile = step - pairs
        x_tile = x_ref.at[pl.ds(pl.multiple_of(jnp.minimum(tile, x_ref.shape[0] // BLOCK - 1) * BLOCK, BLOCK), BLOCK)]
        low_tile = low_ref.at[pl.ds(pl.multiple_of(jnp.minimum(tile, BLOCKS - 1) * BLOCK, BLOCK), BLOCK)]
        weight_refs = (gain_ref, shift_ref, up_ref, up_bias_ref, down_ref, down_bias_ref)
        if top:
            ff_bwd_body(layer, True, 0, parts, tile, id_ref, x_tile, low_tile, g_ref, low_t_ref, *weight_refs, wo_ref,
                        out_ref, mid_g_ref, att_g_ref, small_ref, up_bias_g_ref, kept_ref, *ff_scratch)
        else:
            ff_fwd_body(layer, tile, x_tile, low_tile, wo_ref, *weight_refs, out_ref, mid_ref)


def layer_forward(layer, lengths, ids, parts, quarters, x, gains, shifts, w, fm, wo, up, up_bias, down, down_bias, grad=None, after=()):
    length, width = x.shape
    hidden = up.shape[2]
    pairs = fm.shape[1] // 2
    heads = 2 * pairs
    tiles = length // BLOCK
    top = grad is not None
    pair = lambda i: jnp.minimum(i, pairs - 1)
    tile = lambda i: jnp.clip(i - pairs, 0, tiles - 1)
    per_pair = pl.BlockSpec((1, LIVE, LANES), lambda i, *_: (pair(i), 0, 0))
    per_head = pl.BlockSpec((2, LIVE, 256), lambda i, *_: (pair(i), 0, 0))
    rows = pl.BlockSpec((BLOCK, width), lambda i, *_: (tile(i), 0))
    live = pl.BlockSpec((BLOCK, width), lambda i, *_: (jnp.minimum(tile(i), BLOCKS - 1), 0))
    out_specs = [resident(width, LIVE), per_head, per_head] + [per_pair] * 5
    out_shape = [jax.ShapeDtypeStruct((width, LIVE), BF16)] + [jax.ShapeDtypeStruct((heads, LIVE, 256), BF16)] * 2
    out_shape += [jax.ShapeDtypeStruct((pairs, LIVE, LANES), dtype) for dtype in (F32, F32, BF16, F32, F32)]
    scratch = [
        pltpu.VMEM((LIVE, width), BF16),
        pltpu.VMEM((3, pairs, LIVE, LANES), F32),
        pltpu.VMEM((BLOCKS, BLOCK, BLOCK), BF16),
        pltpu.VMEM((BLOCKS - 1, REACH, BLOCK), BF16),
        pltpu.VMEM((2, BLOCK, 256), F32),
        pltpu.VMEM((LIVE, width), BF16),
    ]
    if top:
        end = piece_shapes(parts, quarters, width, hidden)
        group = end[0] // GROUPS
        out_specs += [rows, rows, live, resident(8, width), resident(1, hidden)]
        out_specs.append(pl.BlockSpec((group,) + end[1:], lambda i, *_: (jnp.clip(i - pairs - tiles, 0, 2 * GROUPS - 1), 0, 0, 0)))
        out_shape += [jax.ShapeDtypeStruct(shape, F32) for shape in ((length, width), (length, width), (LIVE, width), (8, width), (1, hidden), (parts,) + end[1:])]
        scratch += [pltpu.VMEM((width, LIVE), BF16)] + ff_bwd_scratch(length, width, hidden, quarters) + [pltpu.VMEM((BLOCK, width), F32)]
    else:
        out_specs += [resident(width, LIVE), rows, rows]
        out_shape += [jax.ShapeDtypeStruct((width, LIVE), BF16)] + [jax.ShapeDtypeStruct((length, width), F32)] * 2
    return call(
        functools.partial(layer_body, layer, top, pairs, parts),
        after,
        grid=(pairs + tiles + (2 * GROUPS if top else 0),),
        prefetch=[lengths, ids],
        operands=[x, gains, shifts, w, fm, wo, up, up_bias, down, down_bias] + ([grad] if top else []),
        in_specs=[
            constant(*x.shape),
            constant(*gains.shape),
            constant(*shifts.shape),
            of_layer(layer, w),
            pl.BlockSpec((None, 2) + fm.shape[2:], lambda i, *_: (layer, pair(i), 0, 0)),
            anywhere(),
            anywhere(),
            constant(*up_bias.shape),
            anywhere(),
            constant(*down_bias.shape),
        ]
        + ([rows] if top else []),
        out_specs=out_specs,
        scratch=scratch + [pltpu.VMEM(array.shape[1:], array.dtype) for array in (wo, up, down)] + [pltpu.SemaphoreType.DMA((3,))],
        out_shape=out_shape,
        us=20.0,
        name="layer_top" if top else "layer_forward",
    )


def input_bwd_body(layer, runs, parts, order, ends, id_ref, *refs):
    left_refs = refs[: 3 * runs]
    w_ref, normed_t_ref, x_ref, gain_ref, mid_g_ref = refs[3 * runs : 3 * runs + 5]
    small_refs = refs[3 * runs + 5 : -4]
    if ends:
        out_ref, small_ref, sent_ref, kept_ref = refs[-4:]
    else:
        out_ref, small_ref = refs[-2:]
    step = pl.program_id(0)
    tiles = pl.num_programs(0) - (2 if ends else 0)

    @pl.when(step == 0)
    def _():
        small_ref[...] = jnp.zeros_like(small_ref)

    @pl.when(step < BLOCKS)
    def _():
        rows = pl.ds(pl.multiple_of(step * BLOCK, BLOCK), BLOCK)
        back = jnp.zeros(x_ref.shape, F32)
        for run in range(runs):
            for j in range(3):
                left = left_refs[3 * run + j]
                wide = left.shape[1]
                back = back + dot_nt(left[rows, :], w_ref[j, :, run * wide : run * wide + wide])
        unit, rstd = normalize(x_ref[...])
        out_ref[...] = mid_g_ref[...] + norm_pull(back, gain_ref[layer, 0:1, :], unit, rstd)
        small_ref[0:1, :] += jnp.sum(back * unit, axis=0, keepdims=True)
        small_ref[1:2, :] += jnp.sum(back, axis=0, keepdims=True)

    @pl.when((step >= BLOCKS) & (step < tiles))
    def _():
        out_ref[...] = mid_g_ref[...]

    if not ends:
        return
    count, quarters = sent_ref.shape[:2]
    ids = (id_ref[0] & (count - 1), id_ref[1])
    for when, flip, end_ref in ((tiles, 1, sent_ref), (tiles + 1, 0, kept_ref)):
        half = (id_ref[0] // (parts // 2)) ^ flip

        @pl.when(step == when)
        def _(half=half, end_ref=end_ref):
            tall = normed_t_ref.shape[0] // 2
            normed_t = normed_t_ref[pl.ds(pl.multiple_of(half * tall, tall), tall), :]
            totals = [jnp.concatenate([dot(normed_t, left_refs[3 * run + j][...]) for run in range(runs)], axis=1) for j in range(3)]
            for quarter in range(quarters):
                put(end_ref, ids, jnp.concatenate([columns(total, quarter) for total in totals], axis=0), quarter, 0)
            base = 3 * tall // count
            if order:
                room = end_ref.shape[2] - base
                end_ref[:, :, base:, :] = jnp.zeros((count, quarters, room, LANES), F32)

                @pl.when(half == 0)
                def _():
                    for at, (array, row, first) in enumerate(order):
                        portion, offset = divmod(at, room)
                        source = small_ref if array < 0 else small_refs[array]
                        per = source.shape[1] // quarters
                        for quarter in range(quarters):
                            start = quarter * per + first
                            end_ref[portion ^ ids[0], quarter ^ ids[1], base + offset : base + offset + 1, :] = source[row : row + 1, start : start + LANES]


def input_bwd(layer, ids, parts, quarters, proj_g, w, normed_t, x, gains, mid_g, smalls=(), order=(), ends=True, after=()):
    length, width = x.shape
    tiles = length // BLOCK
    rows = pl.BlockSpec((BLOCK, width), lambda i, ids: (jnp.minimum(i, tiles - 1), 0))
    lefts = [part for run in proj_g for part in run]
    small_rows = small_rows_of(len(order), parts)
    end = (parts // 2, quarters, 3 * width // parts + small_rows, LANES)
    return call(
        functools.partial(input_bwd_body, layer, len(proj_g), parts, tuple(order), ends),
        after,
        grid=(tiles + (2 if ends else 0),),
        prefetch=[ids],
        operands=lefts + [w, normed_t, x, gains, mid_g] + list(smalls),
        in_specs=[constant(*a.shape) for a in lefts]
        + [of_layer(layer, w), constant(*normed_t.shape), rows, constant(*gains.shape), rows]
        + [constant(*a.shape) for a in smalls],
        out_specs=[rows, resident(8, width)] + [resident(*end)] * (2 if ends else 0),
        out_shape=[jax.ShapeDtypeStruct((length, width), F32), jax.ShapeDtypeStruct((8, width), F32)] + [jax.ShapeDtypeStruct(end, F32)] * (2 if ends else 0),
        us=1.0,
        name="input_backward",
    )


def small_rows_of(count, parts):
    return -(-count // (8 * parts)) * 8


def cut_of(rows):
    return rows // 16 * 8 if rows >= 16 else rows // 2


def fork_body(kept_ref, got_ref, *ends):
    portions = kept_ref.shape[0]
    cut = ends[0].shape[2]
    for slot in range(portions):
        upper, lower = ends[slot // (portions // 2)], ends[2 + slot % 2]
        upper[slot % (portions // 2)] = kept_ref[slot, :, :cut] + got_ref[slot, :, :cut]
        lower[slot // 2] = kept_ref[slot, :, cut:] + got_ref[slot, :, cut:]


def fork(kept, got, after):
    portions, quarters, rows, _ = kept.shape
    cut = cut_of(rows)
    ends = [(portions // 2, quarters, n, LANES) for n in (cut, cut, rows - cut, rows - cut)]
    by_quarter = lambda shape: pl.BlockSpec((shape[0], 1) + shape[2:], lambda i: (0, i, 0, 0))
    return call(
        fork_body,
        after,
        grid=(quarters,),
        prefetch=[],
        operands=[kept, got],
        in_specs=[by_quarter(kept.shape)] * 2,
        out_specs=[by_quarter(end) for end in ends],
        out_shape=[jax.ShapeDtypeStruct(end, F32) for end in ends],
        us=3.0,
        name="fork_terms",
    )


def add_body(count, *refs):
    outs = refs[2 * count :]
    for which in range(count):
        for side in range(2):
            outs[2 * which + side][...] = refs[2 * which][:, side] + refs[2 * which + 1][:, side]


def add_streams(streams, wheres, after):
    operands, shapes = [], []
    for pair, where in zip(streams, wheres):
        shape = pair[0].shape
        flat = (math.prod(shape[:where]), 2, math.prod(shape[where + 1 : -2])) + shape[-2:]
        operands += [part.reshape(flat) for part in pair]
        shapes.append((flat[0],) + flat[2:])
    outs = [shape for shape in shapes for _ in range(2)]
    got = call(
        functools.partial(add_body, len(streams)),
        after,
        grid=(1,),
        prefetch=[],
        operands=operands,
        in_specs=[constant(*a.shape) for a in operands],
        out_specs=[resident(*shape) for shape in outs],
        out_shape=[jax.ShapeDtypeStruct(shape, F32) for shape in outs],
        us=1.5,
        name="add_terms",
    )
    results = []
    for which in range(len(got) // 2):
        shape, where = streams[which][0].shape, wheres[which]
        lead = shape[:where] + shape[where + 1 : -2]
        results.append(tuple(part.reshape(lead + part.shape[-2:]) for part in got[2 * which : 2 * which + 2]))
    return results


def last_add_body(counts, *refs):
    upper_ref, lower_ref = refs[-2:]
    cut = upper_ref.shape[0]
    first, base = 0, 0
    for count in counts:
        total = sum(ref[...] for ref in refs[first : first + count])
        first += count
        rows = total.shape[0]
        split = min(max(cut - base, 0), rows)
        if split:
            upper_ref[base : base + split, :] = total[:split]
        if split < rows:
            lower_ref[base + split - cut : base + rows - cut, :] = total[split:]
        base += rows


def last_add(runs, after):
    operands = [term for run in runs for term in run]
    rows = sum(run[0].shape[0] for run in runs)
    cut = cut_of(rows)
    return call(
        functools.partial(last_add_body, tuple(len(run) for run in runs)),
        after,
        grid=(1,),
        prefetch=[],
        operands=operands,
        in_specs=[constant(*a.shape) for a in operands],
        out_specs=[resident(cut, LANES), resident(rows - cut, LANES)],
        out_shape=[jax.ShapeDtypeStruct((cut, LANES), F32), jax.ShapeDtypeStruct((rows - cut, LANES), F32)],
        us=1.5,
        name="last_terms",
    )


def hold_body(*refs):
    del refs


def hold(block, after):
    return call(
        hold_body,
        after,
        grid=(1,),
        prefetch=[],
        operands=[block],
        in_specs=[pl.BlockSpec(memory_space=pl.ANY)],
        out_specs=pl.BlockSpec(memory_space=pl.ANY),
        out_shape=jax.ShapeDtypeStruct(block.shape, block.dtype),
        aliases=[(0, 0)],
        us=1.0,
        name="hold",
    )


def swap(block, axis_name, bit):
    return lax.ppermute(block, axis_name, [(i, i ^ bit) for i in range(lax.axis_size(axis_name))])


def bits_of(extent):
    return [1 << i for i in range(extent.bit_length() - 1)]


class Line:
    def __init__(self):
        self.last = []

    def __call__(self, function, *args, **kwargs):
        made = function(*args, after=self.last, **kwargs)
        leaves = jax.tree.leaves(made)
        self.last = [min(leaves, key=lambda a: a.size)]
        return made

    def wait(self, *chains):
        self.last = self.last + [array for chain in chains for array in chain.pending]


def scatter(line, sent, kept, parts, quarters):
    dp_bits, batch_bits = bits_of(parts), bits_of(quarters)
    near, far = dp_bits[0], dp_bits[1:]
    got = swap(sent, "dp", near)
    yield [got]
    ends = line(fork, kept, got)
    names = [("dp", bit) for bit in far] + [("batch", bit) for bit in batch_bits[::-1]]
    streams, left = [], []
    for which, order in enumerate((far, far[::-1])):
        kept, sent = ends[2 * which : 2 * which + 2]
        left.append([name for name in names if name != ("dp", order[0])])
        kept, sent = (part.reshape((2,) * len(left[-1]) + part.shape[2:]) for part in (kept, sent))
        streams.append((kept, swap(sent, "dp", order[0])))
    yield [got for _, got in streams]
    orders = (far[1:], far[::-1][1:])
    orders = [[("dp", bit) for bit in order] + [("batch", bit) for bit in last] for order, last in zip(orders, (batch_bits, batch_bits[::-1]))]
    for steps in zip(*orders):
        wheres = [names_left.index(step) for names_left, step in zip(left, steps)]
        results = line(add_streams, streams, wheres)
        for which, step in enumerate(steps):
            left[which].remove(step)
            streams[which] = (results[which][0], swap(results[which][1], *step))
        yield [got for _, got in streams]
    return streams


def spread(halves, parts):
    dp_bits = bits_of(parts)
    near, far = dp_bits[0], dp_bits[1:]
    streams = list(halves)
    names = [[], []]
    for bits in zip(far[::-1], far):
        moved = [swap(stream, "dp", bit) for stream, bit in zip(streams, bits)]
        yield moved
        for which, bit in enumerate(bits):
            names[which].append(bit)
            names[which].sort()
            streams[which] = jnp.stack([streams[which], moved[which]], axis=names[which].index(bit))
    block = jnp.concatenate(streams, axis=-2)
    block = block.reshape(parts // 2, block.shape[-2], LANES)
    moved = swap(block, "dp", near)
    yield [moved]
    return block, moved


class Chain:
    def __init__(self, steps):
        self.steps, self.result, self.pending = steps, None, []

    def step(self):
        if self.result is None:
            try:
                self.pending = next(self.steps)
            except StopIteration as stop:
                self.result = stop.value

    def finish(self):
        while self.result is None:
            self.step()
        return self.result


def unpack_body(names, bases, pieces, inputs, filled, id_ref, *refs):
    out_refs = dict(zip(names, refs[inputs + filled :]))
    down_ref, small_ref = refs[-2:]
    me = id_ref[0] if inputs == 2 else 0
    for top in range(inputs):
        ref = refs[top]
        portions = ref.shape[0]
        for slot in range(portions):
            portion = (slot + top * portions) ^ me
            half = portions * inputs // 2
            upper, inner = portion // half, portion % half
            for name, layer, first, rows in pieces:
                values = ref[slot, first : first + rows, :]
                if name == "small":
                    small_ref[pl.ds(pl.multiple_of(portion * rows, 8), rows), :] = values
                    continue
                out_ref = out_refs[name]
                layer = layer - bases[name]
                if name == "qkv":
                    width = out_ref.shape[1] // 3
                    unit = math.gcd(rows, width // 2)
                    for k in range(0, rows, unit):
                        flat = inner * rows + k
                        start = (flat // (width // 2)) * width + upper * (width // 2) + flat % (width // 2)
                        out_ref[layer, pl.ds(pl.multiple_of(start, 8), unit), :] = values[k : k + unit]
                elif name == "up":
                    height = out_ref.shape[1]
                    flat = portion * rows
                    tile, start = flat // height, flat % height
                    out_ref[layer, pl.ds(pl.multiple_of(start, 8), rows), pl.ds(pl.multiple_of(tile * LANES, LANES), LANES)] = values
                elif name == "down":
                    down_ref[pl.ds(pl.multiple_of(portion * rows, 8), rows), :] = values
                else:
                    out_ref[layer, pl.ds(pl.multiple_of(portion * rows, 8), rows), :] = values
    if "down" in out_refs:
        for first in range(0, down_ref.shape[0], LANES):
            out_refs["down"][0, first : first + LANES, :] = down_ref[first : first + LANES, :].T
    if "gains" in out_refs:
        layers, wide = out_refs["up_bias"].shape
        row = 0
        for layer in range(layers):
            for name, count in (("gains", 2), ("shifts", 2)):
                out_refs[name][layer] = small_ref[row : row + count, :]
                row += count
            for k in range(wide // LANES):
                out_refs["up_bias"][layer : layer + 1, k * LANES : k * LANES + LANES] = small_ref[row : row + 1, :]
                row += 1
            out_refs["down_bias"][layer : layer + 1, :] = small_ref[row : row + 1, :]
            row += 1


def unpack(ids, pair, pieces, layers, width, hidden, quarters, filled=(), after=()):
    shapes = {"down": (layers, hidden, LANES), "up": (layers, width, hidden // quarters), "out": (layers, width, LANES), "qkv": (layers, 3 * width, LANES)}
    found = {name: [layer for piece, layer, _, _ in pieces if piece == name] for name in shapes}
    names = tuple(name for name in shapes if found[name])
    bases = {name: min(found[name]) for name in names}
    out_specs = [
        pl.BlockSpec((len(found[name]),) + shapes[name][1:], lambda *_, name=name: (bases[name] // len(found[name]), 0, 0)) for name in names
    ]
    out_shape = [jax.ShapeDtypeStruct(shapes[name], F32) for name in names]
    small = [rows for piece, _, _, rows in pieces if piece == "small"]
    if small:
        names += ("gains", "shifts", "up_bias", "down_bias")
        for shape in ((layers, 2, LANES), (layers, 2, LANES), (layers, hidden // quarters), (layers, LANES)):
            out_specs.append(resident(*shape))
            out_shape.append(jax.ShapeDtypeStruct(shape, F32))
    return call(
        functools.partial(unpack_body, names, bases, pieces, len(pair), len(filled)),
        after,
        grid=(1,),
        prefetch=[ids],
        operands=list(pair) + list(filled),
        in_specs=[constant(*a.shape) for a in pair] + [pl.BlockSpec(memory_space=pl.ANY)] * len(filled),
        out_specs=out_specs,
        scratch=[
            pltpu.VMEM((hidden if found["down"] else 8, LANES), F32),
            pltpu.VMEM((len(pair) * pair[0].shape[0] * small[0] if small else 8, LANES), F32),
        ],
        out_shape=out_shape,
        aliases=[(len(pair) + which, which) for which in range(len(filled))],
        us=4.0,
        name="unpack",
    )


def reverse_bits(value, extent):
    return sum(((value // bit) % 2) * (extent // (2 * bit)) for bit in bits_of(extent))


def per_device(activations_in, gains, shifts, qkv_weights, out_weights, up_weights, up_bias, down_weights, down_bias, feature_maps, lengths, cotangent):
    layers, _, width = gains.shape
    hidden = up_bias.shape[1]
    parts, quarters = lax.axis_size("dp"), lax.axis_size("batch")
    ids = jnp.stack([reverse_bits(lax.axis_index("dp"), parts), lax.axis_index("batch")]).astype(jnp.int32)
    proteins = lengths[0]
    pairs = feature_maps.shape[1] // 2
    half = pairs // 2
    line = Line()
    last = layers - 1
    weights = (gains, shifts, qkv_weights, feature_maps, out_weights, up_weights, up_bias, down_weights, down_bias)
    x_one = activations_in[0]
    normed_zero_t, *kept_zero, low_t, x_two, mid = layer_forward(0, proteins, ids, parts, quarters, x_one, *weights)
    normed_one_t, *kept_one, values, mid_g, att_g, small_two, up_bias_g, first = layer_forward(1, proteins, ids, parts, quarters, x_two, *weights, grad=cotangent[0])
    line.last = [up_bias_g]
    smalls = [[None, None, None], [None, small_two, up_bias_g]]
    saved = ((x_one, normed_zero_t, kept_zero), (x_two, normed_one_t, kept_one))

    def attn_part(layer, att_g, first, count, us):
        phi_q, phi_k, uq, uk, v, att, rden = saved[layer][2]
        return line(attn_bwd, layer, proteins, att_g, att, rden, phi_q, phi_k, uq, uk, v, feature_maps, first, count, us)

    def input_part(layer, proj_g, mid_g, **rest):
        grad, smalls[layer][0], *ends = line(
            input_bwd, layer, ids, parts, quarters, proj_g, qkv_weights, saved[layer][1], saved[layer][0], gains, mid_g, **rest
        )
        return grad, Chain(scatter(line, *ends, parts, quarters)) if ends else None

    wide = hidden // quarters // LANES
    ff_rows = (hidden // parts, width * wide // parts, width // parts)
    ff_total, qkv_rows = sum(ff_rows), 3 * width // parts
    sizes = (layers, width, hidden, quarters)

    def ff_pieces(layer, base):
        return (("down", layer, base, ff_rows[0]), ("up", layer, base + ff_rows[0], ff_rows[1]), ("out", layer, base + ff_rows[0] + ff_rows[1], ff_rows[2]))

    first = lax.psum_scatter(first.reshape(-1, LANES), "dp", scatter_dimension=0, tiled=True)
    runs = [attn_part(1, att_g, 0, pairs, 1.0)]
    grad, _ = input_part(1, runs, mid_g, ends=False)
    mid_g, att_g, smalls[0][1], smalls[0][2], sent, kept = line(
        ff_bwd, 0, ids, parts, quarters, grad, low_t, gains, shifts, up_weights, up_bias, down_weights, out_weights, mid, (normed_one_t, runs)
    )
    second = Chain(scatter(line, sent, kept, parts, quarters))
    second.step()
    runs = [attn_part(0, att_g, 0, half, 60.0)]
    second.step()
    first = lax.psum_scatter(line(hold, first), "batch", scatter_dimension=0, tiled=True)
    runs.append(attn_part(0, att_g, half, pairs - half, 1.0))
    flat = [array for layer in range(layers) for array in smalls[layer]]
    order = []
    for layer in range(layers):
        one, two, bias = (3 * layer + k for k in range(3))
        order += [(one, 0, 0), (two, 0, 0), (one, 1, 0), (two, 1, 0)] + [(bias, 0, k * LANES) for k in range(wide)] + [(two, 2, 0)]
    present = [k for k, array in enumerate(flat) if array is not None]
    order = [(present.index(array) if array in present else -1, row, first_col) for array, row, first_col in order]
    grad, third = input_part(0, runs, mid_g, smalls=[flat[k] for k in present], order=order)
    third.step()
    second.step()
    third.step()
    second.step()
    first = lax.all_gather(line(hold, first), "dp", tiled=True).reshape(parts, -1, LANES)
    third.step()
    third.step()
    second.step()
    third.step()
    down, up, out = line(unpack, ids, [first], ff_pieces(1, 0), *sizes)
    pair = Chain(spread(line(last_add, second.finish() + third.finish()), parts)).finish()
    pieces = ff_pieces(0, 0) + (("qkv", 1, ff_total, qkv_rows), ("qkv", 0, ff_total + qkv_rows, qkv_rows))
    pieces += (("small", 0, ff_total + 2 * qkv_rows, small_rows_of(len(order), parts)),)
    down, up, out, qkv, gains_g, shifts_g, up_bias_g, down_bias_g = line(unpack, ids, pair, pieces, *sizes, (down, up, out))
    return (
        values[None],
        grad[None],
        gains_g,
        shifts_g,
        qkv.reshape(layers, 3, width, LANES),
        out,
        up,
        up_bias_g,
        down,
        down_bias_g,
    )


def solution(mesh):
    rows = P(("dp", "batch"), None, None)
    return jax.shard_map(
        per_device,
        mesh=mesh,
        in_specs=(rows,) + (P(),) * 9 + (P(("dp", "batch"), None), rows),
        out_specs=(
            rows,
            rows,
            P(None, None, "batch"),
            P(None, None, "batch"),
            P(None, None, None, "batch"),
            P(None, None, "batch"),
            P(None, None, "batch"),
            P(None, "batch"),
            P(None, None, "batch"),
            P(None, "batch"),
        ),
        check_vma=False,
    )
```

profile of v0, /device:TPU:0, one launch (start us, length us, event | category | flops | bytes accessed | tf_op | source)
XLA Modules:
  0.0 310.2 jit_solution(16178029458985329141)
XLA Ops:
  7.9 25.0 %layer_forward.1 = (bf16[512,768]{1,0:T(8,128)(2,1)}, bf16[8,768,256]{2,1,0:T(8,128)(2,1)}, bf16[8,768,256]{2,1,0:T(8,128)(2,1)}, f32[4,768,128]{2,1,0:T(8,128)}...) custom-call(s32[6]{0:T(128)} %bitcast.82, ...), custom_call_target="tpu_custom_call" | custom-call | flops 23000000512 | tf_op jit(solution)/shard_map/layer_forward/pallas_call | solution.py:42
  32.9 42.8 %layer_top.1 = (bf16[512,768]{1,0:T(8,128)(2,1)}, bf16[8,768,256]{2,1,0:T(8,128)(2,1)}, bf16[8,768,256]{2,1,0:T(8,128)(2,1)}, f32[4,768,128]{2,1,0:T(8,128)}, f3...) custom-call(s32[6]{0:T(128)} %bitcast.83, ...), custom_call_target="tpu_custom_call" | custom-call | flops 23000000512 | tf_op jit(solution)/shard_map/layer_top/pallas_call | solution.py:42
  75.8 20.1 %attn_backward.3 = (bf16[768,512]{1,0:T(8,128)(2,1)}, bf16[768,512]{1,0:T(8,128)(2,1)}, bf16[768,512]{1,0:T(8,128)(2,1)}) custom-call(s32[6]{0:T(128)} %bitcast.84, f32[1,2048]{1,0:T(1,128)} %get-tuple-element.103.refs_1_.refs_17_, f32[768,512]{1,0:T(8,128)} %get-tuple-element.104.refs_2_, f32[4,768,128]{2,1,0:T(8,128)} %get-tuple-element.105.refs_3_, ...), custom_call_target="tpu_custom_call" | custom-call | flops 1150000000 | tf_op jit(solution)/shard_map/attn_backward/pallas_call | solution.py:42
  95.9 7.3 %input_backward.2 = (f32[1024,512]{1,0:T(8,128)}, f32[8,512]{1,0:T(8,128)}) custom-call(s32[2]{0:T(128)} %pad_add_fusion.refs_1_.refs_0_, bf16[768,512]{1,0:T(8,128)(2,1)} %get-tuple-element.112.refs_1_.refs_2_.refs_3_, bf16[768,512]{1,0:T(8,128)(2,1)} %get-tuple-element.112.refs_1_.refs_2_.refs_3_, bf16[768,512]{1,0:T(8,128)(2,1)} %get-tuple-element.113.refs_3_.refs_4_, ...), custom_call_target="tpu_custom_call" | custom-call | flops 1150000000 | tf_op jit(solution)/shard_map/input_backward/pallas_call | solution.py:42
  103.1 30.1 %ff_backward.1 = (f32[1024,512]{1,0:T(8,128)}, f32[768,512]{1,0:T(8,128)}, f32[8,512]{1,0:T(8,128)}, f32[1,2048]{1,0:T(1,128)}, f32[4,4,768,128]{3,2,1,0:T(8,128)}, /*index=5*/f32[4,4,768,128]{3,2,1,0:T(8,128)}) custom-call(s32[2]{0:T(128)} %pad_add_fusion.refs_1_.refs_0_, f32[8,512]{1,0:T(8,128)} %get-tuple-element.117.refs_1_.refs_15_, ...), custom_call_target="tpu_custom_call" | custom-call | flops 20700000256 | tf_op jit(solution)/shard_map/ff_backward/pallas_call | solution.py:42
  133.6 12.4 %attn_backward.4 = (bf16[768,256]{1,0:T(8,128)(2,1)}, bf16[768,256]{1,0:T(8,128)(2,1)}, bf16[768,256]{1,0:T(8,128)(2,1)}) custom-call(s32[6]{0:T(128)} %bitcast.85, f32[1,2048]{1,0:T(1,128)} %get-tuple-element.121.refs_1_.refs_14_, f32[768,512]{1,0:T(8,128)} %get-tuple-element.122.refs_2_, f32[4,768,128]{2,1,0:T(8,128)} %get-tuple-element.123.refs_3_, ...), custom_call_target="tpu_custom_call" | custom-call | flops 69000003584 | tf_op jit(solution)/shard_map/attn_backward/pallas_call | solution.py:42
  146.0 7.4 %fork_terms.2 = (f32[2,4,384,128]{3,2,1,0:T(8,128)}, f32[2,4,384,128]{3,2,1,0:T(8,128)}, f32[2,4,384,128]{3,2,1,0:T(8,128)}, f32[2,4,384,128]{3,2,1,0:T(8,128)}) custom-call(bf16[768,256]{1,0:T(8,128)(2,1)} %get-tuple-element.130.refs_0_.refs_2_, f32[4,4,768,128]{3,2,1,0:T(8,128)} %get-tuple-element.131.refs_1_, f32[4,4,768,128]{3,2,1,0:T(8,128)} %collective-permute-done.refs_2_), custom_call_target="tpu_custom_call" | custom-call | flops 3449999872 | tf_op jit(solution)/shard_map/fork_terms/pallas_call | solution.py:42
  153.4 2.2 collective-permute-start.1
  157.2 12.2 %attn_backward.5 = (bf16[768,256]{1,0:T(8,128)(2,1)}, bf16[768,256]{1,0:T(8,128)(2,1)}, bf16[768,256]{1,0:T(8,128)(2,1)}) custom-call(s32[6]{0:T(128)} %bitcast.86, f32[2304,128]{1,0:T(8,128)} %hold.2.refs_1_, f32[768,512]{1,0:T(8,128)} %get-tuple-element.122.refs_2_, f32[4,768,128]{2,1,0:T(8,128)} %get-tuple-element.123.refs_3_, ...), custom_call_target="tpu_custom_call" | custom-call | flops 1150000000 | tf_op jit(solution)/shard_map/attn_backward/pallas_call | solution.py:42
  169.4 11.0 %input_backward.3 = (f32[1024,512]{1,0:T(8,128)}, f32[8,512]{1,0:T(8,128)}, f32[4,4,200,128]{3,2,1,0:T(8,128)}, f32[4,4,200,128]{3,2,1,0:T(8,128)}) custom-call(s32[2]{0:T(128)} %pad_add_fusion.refs_1_.refs_0_, bf16[768,256]{1,0:T(8,128)(2,1)} %get-tuple-element.135.refs_1_.refs_5_, bf16[768,256]{1,0:T(8,128)(2,1)} %get-tuple-element.130.refs_0_.refs_2_, ...), custom_call_target="tpu_custom_call" | custom-call | flops 1150000000 | tf_op jit(solution)/shard_map/input_backward/pallas_call | solution.py:42
  180.5 10.5 %collective-permute-done.1 = f32[2,2,2,384,128]{4,3,2,1,0:T(8,128)} collective-permute-done((f32[2,2,2,384,128]{4,3,2,1,0:T(8,128)}, f32[2,2,2,384,128]{4,3,2,1,0:T(8,128)}, u32[]{:S(2)}, u32[]{:S(2)}) %collective-permute-start.1) | collective-permute-done | bytes 1572896 | tf_op jit(solution)/shard_map/ppermute | solution.py:837
  192.5 4.6 %add_terms.6 = (f32[1,4,384,128]{3,2,1,0:T(8,128)}, f32[1,4,384,128]{3,2,1,0:T(8,128)}, f32[1,4,384,128]{3,2,1,0:T(8,128)}, f32[1,4,384,128]{3,2,1,0:T(8,128)}) custom-call(f32[8,512]{1,0:T(8,128)} %get-tuple-element.145.refs_0_, f32[1,2,4,384,128]{4,3,2,1,0:T(8,128)} %bitcast.90, f32[1,2,4,384,128]{4,3,2,1,0:T(8,128)} %bitcast.10.refs_2_, ...), custom_call_target="tpu_custom_call" | custom-call | flops 1724999936 | tf_op jit(solution)/shard_map/add_terms/pallas_call | solution.py:42
  199.0 3.9 %fork_terms.3 = (f32[2,4,96,128]{3,2,1,0:T(8,128)}, f32[2,4,96,128]{3,2,1,0:T(8,128)}, f32[2,4,104,128]{3,2,1,0:T(8,128)}, f32[2,4,104,128]{3,2,1,0:T(8,128)}) custom-call(f32[2,2,384,128]{3,2,1,0:T(8,128)} %bitcast.117, f32[4,4,200,128]{3,2,1,0:T(8,128)} %get-tuple-element.150.refs_1_, f32[4,4,200,128]{3,2,1,0:T(8,128)} %collective-permute-done.3.refs_2_), custom_call_target="tpu_custom_call" | custom-call | flops 3449999872 | tf_op jit(solution)/shard_map/fork_terms/pallas_call | solution.py:42
  202.9 13.2 %collective-permute-done.4 = f32[2,2,384,128]{3,2,1,0:T(8,128)S(1)} collective-permute-done((f32[2,2,384,128]{3,2,1,0:T(8,128)}, f32[2,2,384,128]{3,2,1,0:T(8,128)S(1)}, u32[]{:S(2)}, u32[]{:S(2)}) %collective-permute-start.4) | collective-permute-done | bytes 786464 | tf_op jit(solution)/shard_map/ppermute | solution.py:837
  217.1 3.1 add_terms.7
  223.0 1.6 collective-permute-start.10
  224.6 2.5 collective-permute-start.11
  227.1 6.6 %collective-permute-done.6 = f32[2,2,2,96,128]{4,3,2,1,0:T(8,128)S(1)} collective-permute-done((f32[2,2,2,96,128]{4,3,2,1,0:T(8,128)}, f32[2,2,2,96,128]{4,3,2,1,0:T(8,128)S(1)}, u32[]{:S(2)}, u32[]{:S(2)}) %collective-permute-start.6) | collective-permute-done | bytes 393248 | tf_op jit(solution)/shard_map/ppermute | solution.py:837
  235.2 2.3 add_terms.8
  237.5 2.0 collective-permute-start.9
  239.6 9.7 %collective-permute-done.8 = f32[2,2,96,128]{3,2,1,0:T(8,128)S(1)} collective-permute-done((f32[2,2,96,128]{3,2,1,0:T(8,128)}, f32[2,2,96,128]{3,2,1,0:T(8,128)S(1)}, u32[]{:S(2)}, u32[]{:S(2)}) %collective-permute-start.8) | collective-permute-done | bytes 196640 | tf_op jit(solution)/shard_map/ppermute | solution.py:837
  250.0 2.0 add_terms.9
  253.4 2.7 collective-permute-start.13
  256.1 2.2 add_terms.10
  261.0 1.8 add_terms.11
  262.8 1.6 collective-permute-start.16
  266.0 4.1 %unpack.2 = (f32[2,2048,128]{2,1,0:T(8,128)}, f32[2,512,512]{2,1,0:T(8,128)}, f32[2,512,128]{2,1,0:T(8,128)}) custom-call(s32[2]{0:T(128)} %pad_add_fusion.refs_1_.refs_0_, f32[96,128]{1,0:T(8,128)} %bitcast.135, f32[8,576,128]{2,1,0:T(8,128)} %bitcast.87), custom_call_target="tpu_custom_call" | custom-call | flops 4600000000 | tf_op jit(solution)/shard_map/unpack/pallas_call | solution.py:42
  270.9 2.0 last_terms.1
  273.3 6.0 %collective-permute-done.20 = f32[488,128]{1,0:T(8,128)S(1)} collective-permute-done((f32[488,128]{1,0:T(8,128)}, f32[488,128]{1,0:T(8,128)S(1)}, u32[]{:S(2)}, u32[]{:S(2)}) %collective-permute-start.20) | collective-permute-done | bytes 249888 | tf_op jit(solution)/shard_map/ppermute | solution.py:837
  283.5 7.9 %collective-permute-done.19 = f32[2,480,128]{2,1,0:T(8,128)S(1)} collective-permute-done((f32[2,480,128]{2,1,0:T(8,128)S(1)}, f32[2,480,128]{2,1,0:T(8,128)S(1)}, u32[]{:S(2)}, u32[]{:S(2)}) %collective-permute-start.19) | collective-permute-done | bytes 491552 | tf_op jit(solution)/shard_map/ppermute | solution.py:837
  293.0 4.0 %collective-permute-done.22.refs_3_ = f32[4,968,128]{2,1,0:T(8,128)S(1)} collective-permute-done((f32[4,968,128]{2,1,0:T(8,128)S(1)}, f32[4,968,128]{2,1,0:T(8,128)S(1)}, u32[]{:S(2)}, u32[]{:S(2)}) %collective-permute-start.22) | collective-permute-done | bytes 1982496 | tf_op jit(solution)/shard_map/ppermute | solution.py:837
  298.3 5.2 %unpack.3 = (f32[2,2048,128]{2,1,0:T(8,128)}, f32[2,512,512]{2,1,0:T(8,128)}, f32[2,512,128]{2,1,0:T(8,128)}, f32[2,1536,128]{2,1,0:T(8,128)}, f32[2,2,128]{2,1,...) custom-call(s32[2]{0:T(128)} %pad_add_fusion.refs_1_.refs_0_, ...), custom_call_target="tpu_custom_call", output_to_operand_aliasing={{0}: (4, {}), {1}: (5, {}), {2}: (6, {})} | custom-call | flops 4600000000 | tf_op jit(solution)/shard_map/unpack/pallas_call | solution.py:42
  (77 shorter events, 26.1 us)
Async XLA Ops:
  7.2 149.9 %reduce-scatter.3.cloned.1.call-start = ((), (), s32[]{:S(2)}) async-start(), calls=%async_computation.2 | async-start | bytes 10616832 | tf_op jit(solution)/shard_map/reduce_scatter | solution.py:1045
  75.7 144.4 %reduce-scatter.5.cloned.1.call-start = ((), (), s32[]{:S(2)}) async-start(), calls=%async_computation.3 | async-start | bytes 1474560 | tf_op jit(solution)/shard_map/reduce_scatter | solution.py:1055
  133.2 12.8 %collective-permute-start = (f32[4,4,768,128]{3,2,1,0:T(8,128)}, f32[4,4,768,128]{3,2,1,0:T(8,128)}, u32[]{:S(2)}, u32[]{:S(2)}) collective-permute-start(f32[4,4,768,128]{3,2,1,0:T(8,128)} %get-tuple-element.132), channel_id=1, source_target_pairs={{0,4},{4,0},{8,12},{12,8},{16,20},{20,16},{24,28},{28,24},{1,5},{5... | collective-permute-start | bytes 18874376 | tf_op jit(solution)/shard_map/ppermute | solution.py:837
  153.4 37.6 %collective-permute-start.1 = (f32[2,2,2,384,128]{4,3,2,1,0:T(8,128)}, f32[2,2,2,384,128]{4,3,2,1,0:T(8,128)}, u32[]{:S(2)}, u32[]{:S(2)}) collective-permute-start(f32[2,2,2,384,128]{4,3,2,1,0:T(8,128)} %bitcast.93), channel_id=1, source_target_pairs={{0,8},{4,12},{8,0},{12,4},{16,24},{20,28},{24,16},{28,20},{1,9},{5... | collective-permute-start | bytes 4718600 | tf_op jit(solution)/shard_map/ppermute | solution.py:837
  155.7 36.8 %collective-permute-start.2 = (f32[2,2,2,384,128]{4,3,2,1,0:T(8,128)}, f32[2,2,2,384,128]{4,3,2,1,0:T(8,128)}, u32[]{:S(2)}, u32[]{:S(2)}) collective-permute-start(f32[2,2,2,384,128]{4,3,2,1,0:T(8,128)} %bitcast.92), channel_id=1, source_target_pairs={{0,16},{4,20},{8,24},{12,28},{16,0},{20,4},{24,8},{28,12},{1,17},{... | collective-permute-start | bytes 4718600 | tf_op jit(solution)/shard_map/ppermute | solution.py:837
  157.1 108.8 %all-gather.2.cloned.1.call-start = ((), (), s32[]{:S(2)}) async-start(), calls=%async_computation.4 | async-start | bytes 2654208 | tf_op jit(solution)/shard_map/all_gather | solution.py:1069
  180.5 18.5 %collective-permute-start.3 = (f32[4,4,200,128]{3,2,1,0:T(8,128)}, f32[4,4,200,128]{3,2,1,0:T(8,128)}, u32[]{:S(2)}, u32[]{:S(2)}) collective-permute-start(f32[4,4,200,128]{3,2,1,0:T(8,128)} %get-tuple-element.151), channel_id=1, source_target_pairs={{0,4},{4,0},{8,12},{12,8},{16,20},{20,16},{24,28},{28,24},{1,5},{5... | collective-permute-start | bytes 4915208 | tf_op jit(solution)/shard_map/ppermute | solution.py:837
  197.1 19.0 %collective-permute-start.4 = (f32[2,2,384,128]{3,2,1,0:T(8,128)}, f32[2,2,384,128]{3,2,1,0:T(8,128)S(1)}, u32[]{:S(2)}, u32[]{:S(2)}) collective-permute-start(f32[2,2,384,128]{3,2,1,0:T(8,128)} %bitcast.96), channel_id=1, source_target_pairs={{0,16},{4,20},{8,24},{12,28},{16,0},{20,4},{24,8},{28,12},{1,17},{... | collective-permute-start | bytes 2359304 | tf_op jit(solution)/shard_map/ppermute | solution.py:837
  198.4 18.7 %collective-permute-start.5 = (f32[2,2,384,128]{3,2,1,0:T(8,128)}, f32[2,2,384,128]{3,2,1,0:T(8,128)}, u32[]{:S(2)}, u32[]{:S(2)}) collective-permute-start(f32[2,2,384,128]{3,2,1,0:T(8,128)} %bitcast.94), channel_id=1, source_target_pairs={{0,8},{4,12},{8,0},{12,4},{16,24},{20,28},{24,16},{28,20},{1,9},{5... | collective-permute-start | bytes 2359304 | tf_op jit(solution)/shard_map/ppermute | solution.py:837
  216.1 1.0 copy-start.2
  220.2 1.0 copy-start.3
  221.2 12.6 %collective-permute-start.7 = (f32[2,2,2,104,128]{4,3,2,1,0:T(8,128)S(1)}, f32[2,2,2,104,128]{4,3,2,1,0:T(8,128)S(1)}, u32[]{:S(2)}, u32[]{:S(2)}) collective-permute-start(f32[2,2,2,104,128]{4,3,2,1,0:T(8,128)S(1)} %bitcast.97), channel_id=1, source_target_pairs={{0,16},{4,20},{8,24},{12,28},{16,0},{20,4},{24,8},{28,12},{1,17},{... | collective-permute-start | bytes 1277960 | tf_op jit(solution)/shard_map/ppermute | solution.py:837
  222.2 11.5 %collective-permute-start.6 = (f32[2,2,2,96,128]{4,3,2,1,0:T(8,128)}, f32[2,2,2,96,128]{4,3,2,1,0:T(8,128)S(1)}, u32[]{:S(2)}, u32[]{:S(2)}) collective-permute-start(f32[2,2,2,96,128]{4,3,2,1,0:T(8,128)} %bitcast.101), channel_id=1, source_target_pairs={{0,8},{4,12},{8,0},{12,4},{16,24},{20,28},{24,16},{28,20},{1,9},{5... | collective-permute-start | bytes 1179656 | tf_op jit(solution)/shard_map/ppermute | solution.py:837
  223.0 33.1 %collective-permute-start.10 = (f32[2,384,128]{2,1,0:T(8,128)}, f32[2,384,128]{2,1,0:T(8,128)}, u32[]{:S(2)}, u32[]{:S(2)}) collective-permute-start(f32[2,384,128]{2,1,0:T(8,128)} %bitcast.100), channel_id=1, source_target_pairs={{0,1},{1,0},{2,3},{3,2},{4,5},{5,4},{6,7},{7,6},{8,9},{9,8},{10,11... | collective-permute-start | bytes 1179656 | tf_op jit(solution)/shard_map/ppermute | solution.py:837
  224.6 31.5 %collective-permute-start.11 = (f32[2,384,128]{2,1,0:T(8,128)}, f32[2,384,128]{2,1,0:T(8,128)}, u32[]{:S(2)}, u32[]{:S(2)}) collective-permute-start(f32[2,384,128]{2,1,0:T(8,128)} %bitcast.99), channel_id=1, source_target_pairs={{0,2},{1,3},{2,0},{3,1},{4,6},{5,7},{6,4},{7,5},{8,10},{9,11},{10,... | collective-permute-start | bytes 1179656 | tf_op jit(solution)/shard_map/ppermute | solution.py:837
  234.5 0.8 copy-start.4
  237.5 11.8 %collective-permute-start.9 = (f32[2,2,104,128]{3,2,1,0:T(8,128)}, f32[2,2,104,128]{3,2,1,0:T(8,128)S(1)}, u32[]{:S(2)}, u32[]{:S(2)}) collective-permute-start(f32[2,2,104,128]{3,2,1,0:T(8,128)} %bitcast.104), channel_id=1, source_target_pairs={{0,8},{4,12},{8,0},{12,4},{16,24},{20,28},{24,16},{28,20},{1,9},{5... | collective-permute-start | bytes 638984 | tf_op jit(solution)/shard_map/ppermute | solution.py:837
  239.5 9.8 %collective-permute-start.8 = (f32[2,2,96,128]{3,2,1,0:T(8,128)}, f32[2,2,96,128]{3,2,1,0:T(8,128)S(1)}, u32[]{:S(2)}, u32[]{:S(2)}) collective-permute-start(f32[2,2,96,128]{3,2,1,0:T(8,128)} %bitcast.108), channel_id=1, source_target_pairs={{0,16},{4,20},{8,24},{12,28},{16,0},{20,4},{24,8},{28,12},{1,17},{... | collective-permute-start | bytes 589832 | tf_op jit(solution)/shard_map/ppermute | solution.py:837
  252.0 7.2 %collective-permute-start.12 = (f32[2,96,128]{2,1,0:T(8,128)}, f32[2,96,128]{2,1,0:T(8,128)S(1)}, u32[]{:S(2)}, u32[]{:S(2)}) collective-permute-start(f32[2,96,128]{2,1,0:T(8,128)} %bitcast.112), channel_id=1, source_target_pairs={{0,1},{1,0},{2,3},{3,2},{4,5},{5,4},{6,7},{7,6},{8,9},{9,8},{10,11... | collective-permute-start | bytes 294920 | tf_op jit(solution)/shard_map/ppermute | solution.py:837
  253.4 7.0 %collective-permute-start.13 = (f32[2,104,128]{2,1,0:T(8,128)}, f32[2,104,128]{2,1,0:T(8,128)S(1)}, u32[]{:S(2)}, u32[]{:S(2)}) collective-permute-start(f32[2,104,128]{2,1,0:T(8,128)} %bitcast.109), channel_id=1, source_target_pairs={{0,2},{1,3},{2,0},{3,1},{4,6},{5,7},{6,4},{7,5},{8,10},{9,11},{10,... | collective-permute-start | bytes 319496 | tf_op jit(solution)/shard_map/ppermute | solution.py:837
  258.3 11.7 %collective-permute-start.14 = (f32[384,128]{1,0:T(8,128)}, f32[384,128]{1,0:T(8,128)S(1)}, u32[]{:S(2)}, u32[]{:S(2)}) collective-permute-start(f32[384,128]{1,0:T(8,128)} %bitcast.106), channel_id=1, source_target_pairs={{0,2},{1,3},{2,0},{3,1},{4,6},{5,7},{6,4},{7,5},{8,10},{9,11},{10,... | collective-permute-start | bytes 589832 | tf_op jit(solution)/shard_map/ppermute | solution.py:837
  258.6 11.5 %collective-permute-start.15 = (f32[384,128]{1,0:T(8,128)}, f32[384,128]{1,0:T(8,128)S(1)}, u32[]{:S(2)}, u32[]{:S(2)}) collective-permute-start(f32[384,128]{1,0:T(8,128)} %bitcast.105), channel_id=1, source_target_pairs={{0,1},{1,0},{2,3},{3,2},{4,5},{5,4},{6,7},{7,6},{8,9},{9,8},{10,11... | collective-permute-start | bytes 589832 | tf_op jit(solution)/shard_map/ppermute | solution.py:837
  259.2 1.2 copy-start.11
  262.8 7.3 %collective-permute-start.16 = (f32[96,128]{1,0:T(8,128)}, f32[96,128]{1,0:T(8,128)S(1)}, u32[]{:S(2)}, u32[]{:S(2)}) collective-permute-start(f32[96,128]{1,0:T(8,128)} %bitcast.114), channel_id=1, source_target_pairs={{0,2},{1,3},{2,0},{3,1},{4,6},{5,7},{6,4},{7,5},{8,10},{9,11},{10,... | collective-permute-start | bytes 147464 | tf_op jit(solution)/shard_map/ppermute | solution.py:837
  264.4 5.7 %collective-permute-start.17 = (f32[104,128]{1,0:T(8,128)}, f32[104,128]{1,0:T(8,128)S(1)}, u32[]{:S(2)}, u32[]{:S(2)}) collective-permute-start(f32[104,128]{1,0:T(8,128)} %bitcast.113), channel_id=1, source_target_pairs={{0,1},{1,0},{2,3},{3,2},{4,5},{5,4},{6,7},{7,6},{8,9},{9,8},{10,11... | collective-permute-start | bytes 159752 | tf_op jit(solution)/shard_map/ppermute | solution.py:837
  272.9 6.5 %collective-permute-start.20 = (f32[488,128]{1,0:T(8,128)}, f32[488,128]{1,0:T(8,128)S(1)}, u32[]{:S(2)}, u32[]{:S(2)}) collective-permute-start(f32[488,128]{1,0:T(8,128)} %get-tuple-element.181), channel_id=1, source_target_pairs={{0,8},{4,12},{8,0},{12,4},{16,24},{20,28},{24,16},{28,20},{1,9},{5... | collective-permute-start | bytes 749576 | tf_op jit(solution)/shard_map/ppermute | solution.py:837
  273.3 8.1 %collective-permute-start.18 = (f32[480,128]{1,0:T(8,128)}, f32[480,128]{1,0:T(8,128)S(1)}, u32[]{:S(2)}, u32[]{:S(2)}) collective-permute-start(f32[480,128]{1,0:T(8,128)} %get-tuple-element.180.refs_1_), channel_id=1, source_target_pairs={{0,16},{4,20},{8,24},{12,28},{16,0},{20,4},{24,8},{28,12},{1,17},{... | collective-permute-start | bytes 737288 | tf_op jit(solution)/shard_map/ppermute | solution.py:837
  280.4 11.0 %collective-permute-start.21 = (f32[2,488,128]{2,1,0:T(8,128)S(1)}, f32[2,488,128]{2,1,0:T(8,128)S(1)}, u32[]{:S(2)}, u32[]{:S(2)}) collective-permute-start(f32[2,488,128]{2,1,0:T(8,128)S(1)} %get-tuple-element.193), channel_id=1, source_target_pairs={{0,16},{4,20},{8,24},{12,28},{16,0},{20,4},{24,8},{28,12},{1,17},{... | collective-permute-start | bytes 1499144 | tf_op jit(solution)/shard_map/ppermute | solution.py:837
  282.5 8.9 %collective-permute-start.19 = (f32[2,480,128]{2,1,0:T(8,128)S(1)}, f32[2,480,128]{2,1,0:T(8,128)S(1)}, u32[]{:S(2)}, u32[]{:S(2)}) collective-permute-start(f32[2,480,128]{2,1,0:T(8,128)S(1)} %get-tuple-element.195), channel_id=1, source_target_pairs={{0,8},{4,12},{8,0},{12,4},{16,24},{20,28},{24,16},{28,20},{1,9},{5... | collective-permute-start | bytes 1474568 | tf_op jit(solution)/shard_map/ppermute | solution.py:837
  291.7 1.3 copy-start
  293.0 4.0 %collective-permute-start.22 = (f32[4,968,128]{2,1,0:T(8,128)S(1)}, f32[4,968,128]{2,1,0:T(8,128)S(1)}, u32[]{:S(2)}, u32[]{:S(2)}) collective-permute-start(f32[4,968,128]{2,1,0:T(8,128)S(1)} %bitcast.74), channel_id=1, source_target_pairs={{0,4},{4,0},{8,12},{12,8},{16,20},{20,16},{24,28},{28,24},{1,5},{5... | collective-permute-start | bytes 5947400 | tf_op jit(solution)/shard_map/ppermute | solution.py:837
  297.0 1.3 copy-start.1
  (8 other events, 5.5 us)
Sparse Core Ops, SparseCore 0:
  75.9 79.1 reduce-scatter.2
  157.4 29.1 reduce-scatter.4
  220.3 31.9 all-gather.1
where the time goes:
time: 315 us; the launch traced here: 310 us
  Pallas kernels  199 us (63%)
  waiting for transfers between devices  61.6 us (20%)
  starting transfers between devices  24.9 us (8%)
  between operations  14.2 us (5%)
  local copies, waits for them, and re-layouts  7.36 us (2%)
    pallas_call x21, Pallas kernels, call(): pl.pallas_call(ordered, grid_spec=pltpu.PrefetchScalarGridSpec(num_scalar...  199 us
    ppermute x23, waiting for transfers between devices, swap(): lax.ppermute(block, axis_name, [(i, i ^ bit) for i in range(lax.axis_size...  61.5 us
    ppermute x23, starting transfers between devices, swap(): lax.ppermute(block, axis_name, [(i, i ^ bit) for i in range(lax.axis_size...  24.8 us
    unnamed x28, local copies, waits for them, and re-layouts  7.23 us
  transfers between devices with their start and end apart: 26, of which 10 were waited for; matrix products, arithmetic and copies ran while one was open for 1% of the time, Pallas kernels for 40%

commit v1 on v0

--- a/solution.py
+++ b/solution.py
@@ -320,7 +320,7 @@
     )
 
 
-GROUPS = 4
+GROUPS = 2
 
 
 def put(out_ref, ids, values, quarter, base):
@@ -690,7 +690,7 @@
     tiles = length // BLOCK
     rows = pl.BlockSpec((BLOCK, width), lambda i, ids: (jnp.minimum(i, tiles - 1), 0))
     lefts = [part for run in proj_g for part in run]
-    small_rows = small_rows_of(len(order), parts)
+    small_rows = small_rows_of(len(order), parts, 3 * width // parts)
     end = (parts // 2, quarters, 3 * width // parts + small_rows, LANES)
     return call(
         functools.partial(input_bwd_body, layer, len(proj_g), parts, tuple(order), ends),
@@ -708,75 +708,66 @@
     )
 
 
-def small_rows_of(count, parts):
-    return -(-count // (8 * parts)) * 8
-
-
-def cut_of(rows):
-    return rows // 16 * 8 if rows >= 16 else rows // 2
-
-
-def fork_body(kept_ref, got_ref, *ends):
-    portions = kept_ref.shape[0]
-    cut = ends[0].shape[2]
-    for slot in range(portions):
-        upper, lower = ends[slot // (portions // 2)], ends[2 + slot % 2]
-        upper[slot % (portions // 2)] = kept_ref[slot, :, :cut] + got_ref[slot, :, :cut]
-        lower[slot // 2] = kept_ref[slot, :, cut:] + got_ref[slot, :, cut:]
-
-
-def fork(kept, got, after):
-    portions, quarters, rows, _ = kept.shape
-    cut = cut_of(rows)
-    ends = [(portions // 2, quarters, n, LANES) for n in (cut, cut, rows - cut, rows - cut)]
-    by_quarter = lambda shape: pl.BlockSpec((shape[0], 1) + shape[2:], lambda i: (0, i, 0, 0))
+def small_rows_of(count, parts, others):
+    least = -(-count // (8 * parts)) * 8
+    return least + (others + least) % 16
+
+
+class Share:
+    def __init__(self, terms, names, rows):
+        self.terms, self.names, self.rows, self.done = terms, names, rows, ()
+
+    def operands(self, step, over):
+        specs = []
+        for _, names, which in self.terms:
+            at = [0 if name in self.done else 1 if name == step else None for name in names]
+            block = [2 if index is None and name not in over else None for name, index in zip(names, at)]
+
+            def index_map(*grid, names=names, at=at, which=which):
+                free = [grid[over.index(name)] if name in over else 0 for name in names]
+                return tuple(one if index is None else index for one, index in zip(free, at)) + (which, 0)
+
+            specs.append(pl.BlockSpec(tuple(block) + (self.rows, LANES), index_map))
+        return [array for array, _, _ in self.terms], specs
+
+    def left(self, step):
+        return [name for name in self.names if name not in self.done and name != step]
+
+    def take(self, step, array):
+        self.terms.append((array, tuple(self.left(step)), 0))
+        self.done += (step,)
+
+
+def sums_body(counts, *refs):
+    outs = refs[len(refs) - len(counts) :]
+    first = 0
+    for count, out in zip(counts, outs):
+        out[...] = sum(ref[...] for ref in refs[first : first + count])
+        first += count
+
+
+def sums_to_send(shares, steps, over, after):
+    operands, in_specs, out_specs, out_shape = [], [], [], []
+    for part, step in zip(shares, steps):
+        arrays, specs = part.operands(step, over)
+        operands += arrays
+        in_specs += specs
+        left = part.left(step)
+        out_shape.append(jax.ShapeDtypeStruct((2,) * len(left) + (part.rows, LANES), F32))
+        block = tuple(None if name in over else 2 for name in left) + (part.rows, LANES)
+        out_specs.append(pl.BlockSpec(block, lambda *grid, left=left: tuple(grid[over.index(n)] if n in over else 0 for n in left) + (0, 0)))
     return call(
-        fork_body,
+        functools.partial(sums_body, tuple(len(part.terms) for part in shares)),
         after,
-        grid=(quarters,),
-        prefetch=[],
-        operands=[kept, got],
-        in_specs=[by_quarter(kept.shape)] * 2,
-        out_specs=[by_quarter(end) for end in ends],
-        out_shape=[jax.ShapeDtypeStruct(end, F32) for end in ends],
-        us=3.0,
-        name="fork_terms",
-    )
-
-
-def add_body(count, *refs):
-    outs = refs[2 * count :]
-    for which in range(count):
-        for side in range(2):
-            outs[2 * which + side][...] = refs[2 * which][:, side] + refs[2 * which + 1][:, side]
-
-
-def add_streams(streams, wheres, after):
-    operands, shapes = [], []
-    for pair, where in zip(streams, wheres):
-        shape = pair[0].shape
-        flat = (math.prod(shape[:where]), 2, math.prod(shape[where + 1 : -2])) + shape[-2:]
-        operands += [part.reshape(flat) for part in pair]
-        shapes.append((flat[0],) + flat[2:])
-    outs = [shape for shape in shapes for _ in range(2)]
-    got = call(
-        functools.partial(add_body, len(streams)),
-        after,
-        grid=(1,),
+        grid=(2,) * len(over) if over else (1,),
         prefetch=[],
         operands=operands,
-        in_specs=[constant(*a.shape) for a in operands],
-        out_specs=[resident(*shape) for shape in outs],
-        out_shape=[jax.ShapeDtypeStruct(shape, F32) for shape in outs],
-        us=1.5,
-        name="add_terms",
+        in_specs=in_specs,
+        out_specs=out_specs,
+        out_shape=out_shape,
+        us=2.0,
+        name="sums_to_send",
     )
-    results = []
-    for which in range(len(got) // 2):
-        shape, where = streams[which][0].shape, wheres[which]
-        lead = shape[:where] + shape[where + 1 : -2]
-        results.append(tuple(part.reshape(lead + part.shape[-2:]) for part in got[2 * which : 2 * which + 2]))
-    return results
 
 
 def last_add_body(counts, *refs):
@@ -795,17 +786,21 @@
         base += rows
 
 
-def last_add(runs, after):
-    operands = [term for run in runs for term in run]
-    rows = sum(run[0].shape[0] for run in runs)
-    cut = cut_of(rows)
+def last_add(shares, after):
+    rows = sum(part.rows for part in shares)
+    cut = rows // 2
+    operands, in_specs = [], []
+    for part in shares:
+        arrays, specs = part.operands(None, ())
+        operands += arrays
+        in_specs += specs
     return call(
-        functools.partial(last_add_body, tuple(len(run) for run in runs)),
+        functools.partial(last_add_body, tuple(len(part.terms) for part in shares)),
         after,
         grid=(1,),
         prefetch=[],
         operands=operands,
-        in_specs=[constant(*a.shape) for a in operands],
+        in_specs=in_specs,
         out_specs=[resident(cut, LANES), resident(rows - cut, LANES)],
         out_shape=[jax.ShapeDtypeStruct((cut, LANES), F32), jax.ShapeDtypeStruct((rows - cut, LANES), F32)],
         us=1.5,
@@ -860,25 +855,20 @@
     near, far = dp_bits[0], dp_bits[1:]
     got = swap(sent, "dp", near)
     yield [got]
-    ends = line(fork, kept, got)
-    names = [("dp", bit) for bit in far] + [("batch", bit) for bit in batch_bits[::-1]]
-    streams, left = [], []
-    for which, order in enumerate((far, far[::-1])):
-        kept, sent = ends[2 * which : 2 * which + 2]
-        left.append([name for name in names if name != ("dp", order[0])])
-        kept, sent = (part.reshape((2,) * len(left[-1]) + part.shape[2:]) for part in (kept, sent))
-        streams.append((kept, swap(sent, "dp", order[0])))
-    yield [got for _, got in streams]
-    orders = (far[1:], far[::-1][1:])
-    orders = [[("dp", bit) for bit in order] + [("batch", bit) for bit in last] for order, last in zip(orders, (batch_bits, batch_bits[::-1]))]
-    for steps in zip(*orders):
-        wheres = [names_left.index(step) for names_left, step in zip(left, steps)]
-        results = line(add_streams, streams, wheres)
-        for which, step in enumerate(steps):
-            left[which].remove(step)
-            streams[which] = (results[which][0], swap(results[which][1], *step))
-        yield [got for _, got in streams]
-    return streams
+    batch_names = [("batch", bit) for bit in batch_bits[::-1]]
+    names = tuple([("dp", bit) for bit in far] + batch_names)
+    rows = kept.shape[2] // 2
+    whole = [part.reshape((2,) * len(names) + part.shape[2:]) for part in (kept, got)]
+    shares = [Share([(part, names, which) for part in whole], names, rows) for which in range(2)]
+    orders = [[("dp", bit) for bit in order] + [("batch", bit) for bit in last] for order, last in ((far, batch_bits), (far[::-1], batch_bits[::-1]))]
+    for count, steps in enumerate(zip(*orders)):
+        large = rows * 2 ** (len(names) - count) > 2**12
+        sums = line(sums_to_send, shares, steps, tuple(batch_names) if large and steps[0][0] == "dp" else ())
+        moved = [swap(block, *step) for block, step in zip(sums, steps)]
+        for part, step, block in zip(shares, steps, moved):
+            part.take(step, block)
+        yield moved
+    return shares
 
 
 def spread(halves, parts):
@@ -997,6 +987,7 @@
         ],
         out_shape=out_shape,
         aliases=[(len(pair) + which, which) for which in range(len(filled))],
+        mib=32,
         us=4.0,
         name="unpack",
     )
@@ -1074,7 +1065,7 @@
     down, up, out = line(unpack, ids, [first], ff_pieces(1, 0), *sizes)
     pair = Chain(spread(line(last_add, second.finish() + third.finish()), parts)).finish()
     pieces = ff_pieces(0, 0) + (("qkv", 1, ff_total, qkv_rows), ("qkv", 0, ff_total + qkv_rows, qkv_rows))
-    pieces += (("small", 0, ff_total + 2 * qkv_rows, small_rows_of(len(order), parts)),)
+    pieces += (("small", 0, ff_total + 2 * qkv_rows, small_rows_of(len(order), parts, qkv_rows)),)
     down, up, out, qkv, gains_g, shifts_g, up_bias_g, down_bias_g = line(unpack, ids, pair, pieces, *sizes, (down, up, out))
     return (
         values[None],

time: 315 us -> 309 us (0.981)
  Pallas kernels: 199 us -> 188 us
  starting transfers between devices: 24.9 us -> 33.5 us
    pallas_call x21, Pallas kernels: 199 us -> 188 us  [call(): pl.pallas_call(ordered, grid_spec=pltpu.PrefetchScalarGridSpec(num_scalar...]
    ppermute x23, starting transfers between devices: 24.8 us -> 33.3 us  [swap(): lax.ppermute(block, axis_name, [(i, i ^ bit) for i in range(lax.axis_size...]
  transfers between devices with their start and end apart: 26 -> 26, of which waited for: 10 -> 14; matrix products, arithmetic and copies ran while one was open for 1% -> 1% of each run, Pallas kernels for 40% -> 38%
where the time goes in v1:
time: 309 us; the launch traced here: 304 us
  Pallas kernels  188 us (61%)
  waiting for transfers between devices  60.1 us (19%)
  starting transfers between devices  33.5 us (11%)
  between operations  14.2 us (5%)
  local copies, waits for them, and re-layouts  5.54 us (2%)
    pallas_call x21, Pallas kernels, call(): pl.pallas_call(ordered, grid_spec=pltpu.PrefetchScalarGridSpec(num_scalar...  188 us
    ppermute x23, waiting for transfers between devices, swap(): lax.ppermute(block, axis_name, [(i, i ^ bit) for i in range(lax.axis_size...  58.5 us
    ppermute x23, starting transfers between devices, swap(): lax.ppermute(block, axis_name, [(i, i ^ bit) for i in range(lax.axis_size...  33.3 us
  transfers between devices with their start and end apart: 26, of which 14 were waited for; matrix products, arithmetic and copies ran while one was open for 1% of the time, Pallas kernels for 38%

profile of v1, /device:TPU:0, one launch (start us, length us, event | category | flops | bytes accessed | tf_op | source)
XLA Modules:
  0.0 303.6 jit_solution(12155728120629407472)
XLA Ops:
  7.9 25.0 %layer_forward.1 = (bf16[512,768]{1,0:T(8,128)(2,1)}, bf16[8,768,256]{2,1,0:T(8,128)(2,1)}, bf16[8,768,256]{2,1,0:T(8,128)(2,1)}, f32[4,768,128]{2,1,0:T(8,128)}...) custom-call(s32[6]{0:T(128)} %bitcast.59, ...), custom_call_target="tpu_custom_call" | custom-call | flops 23000000512 | tf_op jit(solution)/shard_map/layer_forward/pallas_call | solution.py:42
  32.8 41.0 %layer_top.1 = (bf16[512,768]{1,0:T(8,128)(2,1)}, bf16[8,768,256]{2,1,0:T(8,128)(2,1)}, bf16[8,768,256]{2,1,0:T(8,128)(2,1)}, f32[4,768,128]{2,1,0:T(8,128)}, f3...) custom-call(s32[6]{0:T(128)} %bitcast.60, ...), custom_call_target="tpu_custom_call" | custom-call | flops 23000000512 | tf_op jit(solution)/shard_map/layer_top/pallas_call | solution.py:42
  73.9 20.5 %attn_backward.3 = (bf16[768,512]{1,0:T(8,128)(2,1)}, bf16[768,512]{1,0:T(8,128)(2,1)}, bf16[768,512]{1,0:T(8,128)(2,1)}) custom-call(s32[6]{0:T(128)} %bitcast.61, f32[1,2048]{1,0:T(1,128)} %get-tuple-element.87.refs_1_.refs_17_, f32[768,512]{1,0:T(8,128)} %get-tuple-element.88.refs_2_, f32[4,768,128]{2,1,0:T(8,128)} %get-tuple-element.89.refs_3_, ...), custom_call_target="tpu_custom_call" | custom-call | flops 1150000000 | tf_op jit(solution)/shard_map/attn_backward/pallas_call | solution.py:42
  94.4 7.3 %input_backward.2 = (f32[1024,512]{1,0:T(8,128)}, f32[8,512]{1,0:T(8,128)}) custom-call(s32[2]{0:T(128)} %pad_add_fusion.refs_1_.refs_0_, bf16[768,512]{1,0:T(8,128)(2,1)} %get-tuple-element.96.refs_1_.refs_2_.refs_3_, bf16[768,512]{1,0:T(8,128)(2,1)} %get-tuple-element.96.refs_1_.refs_2_.refs_3_, bf16[768,512]{1,0:T(8,128)(2,1)} %get-tuple-element.97.refs_3_.refs_4_, ...), custom_call_target="tpu_custom_call" | custom-call | flops 1150000000 | tf_op jit(solution)/shard_map/input_backward/pallas_call | solution.py:42
  101.7 28.2 %ff_backward.1 = (f32[1024,512]{1,0:T(8,128)}, f32[768,512]{1,0:T(8,128)}, f32[8,512]{1,0:T(8,128)}, f32[1,2048]{1,0:T(1,128)}, f32[4,4,768,128]{3,2,1,0:T(8,128)}, /*index=5*/f32[4,4,768,128]{3,2,1,0:T(8,128)}) custom-call(s32[2]{0:T(128)} %pad_add_fusion.refs_1_.refs_0_, f32[8,512]{1,0:T(8,128)} %get-tuple-element.101.refs_1_.refs_15_, ...), custom_call_target="tpu_custom_call" | custom-call | flops 20700000256 | tf_op jit(solution)/shard_map/ff_backward/pallas_call | solution.py:42
  130.4 12.4 %attn_backward.4 = (bf16[768,256]{1,0:T(8,128)(2,1)}, bf16[768,256]{1,0:T(8,128)(2,1)}, bf16[768,256]{1,0:T(8,128)(2,1)}) custom-call(s32[6]{0:T(128)} %bitcast.62, f32[1,2048]{1,0:T(1,128)} %get-tuple-element.105.refs_1_.refs_14_, f32[768,512]{1,0:T(8,128)} %get-tuple-element.106.refs_2_, f32[4,768,128]{2,1,0:T(8,128)} %get-tuple-element.107.refs_3_, ...), custom_call_target="tpu_custom_call" | custom-call | flops 69000003584 | tf_op jit(solution)/shard_map/attn_backward/pallas_call | solution.py:42
  142.8 5.0 %sums_to_send.8 = (f32[2,2,2,384,128]{4,3,2,1,0:T(8,128)}, f32[2,2,2,384,128]{4,3,2,1,0:T(8,128)}) custom-call(bf16[768,256]{1,0:T(8,128)(2,1)} %get-tuple-element.114.refs_0_.refs_2_, f32[2,2,2,2,768,128]{5,4,3,2,1,0:T(8,128)} %bitcast.31, f32[2,2,2,2,768,128]{5,4,3,2,1,0:T(8,128)} %bitcast.7.refs_2_.refs_4_.refs_5_.refs_6_.refs_7_.refs_8_, ...), custom_call_target="tpu_custom_call" | custom-call | flops 2300000000 | tf_op jit(solution)/shard_map/sums_to_send/pallas_call | solution.py:42
  147.8 2.4 collective-permute-start.2
  153.3 12.2 %attn_backward.5 = (bf16[768,256]{1,0:T(8,128)(2,1)}, bf16[768,256]{1,0:T(8,128)(2,1)}, bf16[768,256]{1,0:T(8,128)(2,1)}) custom-call(s32[6]{0:T(128)} %bitcast.63, f32[2304,128]{1,0:T(8,128)} %hold.2.refs_1_, f32[768,512]{1,0:T(8,128)} %get-tuple-element.106.refs_2_, f32[4,768,128]{2,1,0:T(8,128)} %get-tuple-element.107.refs_3_, ...), custom_call_target="tpu_custom_call" | custom-call | flops 1150000000 | tf_op jit(solution)/shard_map/attn_backward/pallas_call | solution.py:42
  165.5 11.1 %input_backward.3 = (f32[1024,512]{1,0:T(8,128)}, f32[8,512]{1,0:T(8,128)}, f32[4,4,208,128]{3,2,1,0:T(8,128)}, f32[4,4,208,128]{3,2,1,0:T(8,128)}) custom-call(s32[2]{0:T(128)} %pad_add_fusion.refs_1_.refs_0_, bf16[768,256]{1,0:T(8,128)(2,1)} %get-tuple-element.119.refs_1_.refs_5_, bf16[768,256]{1,0:T(8,128)(2,1)} %get-tuple-element.114.refs_0_.refs_2_, ...), custom_call_target="tpu_custom_call" | custom-call | flops 1150000000 | tf_op jit(solution)/shard_map/input_backward/pallas_call | solution.py:42
  176.7 8.8 %collective-permute-done.2.refs_6_.refs_7_.refs_8_.refs_9_ = f32[2,2,2,384,128]{4,3,2,1,0:T(8,128)} collective-permute-done((f32[2,2,2,384,128]{4,3,2,1,0:T(8,128)}, f32[2,2,2,384,128]{4,3,2,1,0:T(8,128)}, u32[]{:S(2)}, u32[]{:S(2)}) %collective-permute-start.2) | collective-permute-done | bytes 1572896 | tf_op jit(solution)/shard_map/ppermute | solution.py:832
  187.0 3.6 %sums_to_send.9 = (f32[2,2,384,128]{3,2,1,0:T(8,128)}, f32[2,2,384,128]{3,2,1,0:T(8,128)}) custom-call(f32[8,512]{1,0:T(8,128)} %get-tuple-element.129.refs_0_, f32[2,2,2,2,768,128]{5,4,3,2,1,0:T(8,128)} %bitcast.33, f32[2,2,2,2,768,128]{5,4,3,2,1,0:T(8,128)} %bitcast.7.refs_2_.refs_4_.refs_5_.refs_6_.refs_7_.refs_8_, ...), custom_call_target="tpu_custom_call" | custom-call | flops 2300000000 | tf_op jit(solution)/shard_map/sums_to_send/pallas_call | solution.py:42
  192.6 2.3 sums_to_send.10
  194.9 14.6 %collective-permute-done.5.refs_8_.refs_9_.refs_10_ = f32[2,2,384,128]{3,2,1,0:T(8,128)S(1)} collective-permute-done((f32[2,2,384,128]{3,2,1,0:T(8,128)}, f32[2,2,384,128]{3,2,1,0:T(8,128)S(1)}, u32[]{:S(2)}, u32[]{:S(2)}) %collective-permute-start.5) | collective-permute-done | bytes 786464 | tf_op jit(solution)/shard_map/ppermute | solution.py:832
  210.9 2.8 sums_to_send.11
  215.5 8.4 %collective-permute-done.7.refs_6_.refs_7_.refs_8_.refs_21_ = f32[2,2,2,104,128]{4,3,2,1,0:T(8,128)S(1)} collective-permute-done((f32[2,2,2,104,128]{4,3,2,1,0:T(8,128)}, f32[2,2,2,104,128]{4,3,2,1,0:T(8,128)S(1)}, u32[]{:S(2)}, u32[]{:S(2)}) %collective-permute-start.7) | collective-permute-done | bytes 426016 | tf_op jit(solution)/shard_map/ppermute | solution.py:832
  223.9 2.2 collective-permute-done.6.refs_3_.refs_15_
  226.9 2.2 sums_to_send.12
  229.0 2.4 collective-permute-start.9
  232.0 3.3 %collective-permute-start.11 = (f32[2,384,128]{2,1,0:T(8,128)}, f32[2,384,128]{2,1,0:T(8,128)S(1)}, u32[]{:S(2)}, u32[]{:S(2)}) collective-permute-start(f32[2,384,128]{2,1,0:T(8,128)} %get-tuple-element.141), channel_id=1, source_target_pairs={{0,2},{1,3},{2,0},{3,1},{4,6},{5,7},{6,4},{7,5},{8,10},{9,11},{10,... | collective-permute-start | bytes 1179656 | tf_op jit(solution)/shard_map/ppermute | solution.py:832
  237.2 2.6 collective-permute-done.8.refs_4_.refs_16_
  239.8 1.9 sums_to_send.13
  241.7 4.2 %collective-permute-start.13 = (f32[2,104,128]{2,1,0:T(8,128)}, f32[2,104,128]{2,1,0:T(8,128)S(1)}, u32[]{:S(2)}, u32[]{:S(2)}) collective-permute-start(f32[2,104,128]{2,1,0:T(8,128)} %get-tuple-element.143), channel_id=1, source_target_pairs={{0,2},{1,3},{2,0},{3,1},{4,6},{5,7},{6,4},{7,5},{8,10},{9,11},{10,... | collective-permute-start | bytes 319496 | tf_op jit(solution)/shard_map/ppermute | solution.py:832
  245.9 2.5 collective-permute-start.12
  252.1 2.4 sums_to_send.14
  254.9 3.1 %collective-permute-start.14 = (f32[384,128]{1,0:T(8,128)}, f32[384,128]{1,0:T(8,128)S(1)}, u32[]{:S(2)}, u32[]{:S(2)}) collective-permute-start(f32[384,128]{1,0:T(8,128)} %get-tuple-element.142.refs_0_), channel_id=1, source_target_pairs={{0,2},{1,3},{2,0},{3,1},{4,6},{5,7},{6,4},{7,5},{8,10},{9,11},{10,... | collective-permute-start | bytes 589832 | tf_op jit(solution)/shard_map/ppermute | solution.py:832
  264.3 2.3 unpack.2
  267.4 2.7 last_terms.1
  271.6 4.9 %collective-permute-done.20 = f32[488,128]{1,0:T(8,128)S(1)} collective-permute-done((f32[488,128]{1,0:T(8,128)}, f32[488,128]{1,0:T(8,128)S(1)}, u32[]{:S(2)}, u32[]{:S(2)}) %collective-permute-start.20) | collective-permute-done | bytes 249888 | tf_op jit(solution)/shard_map/ppermute | solution.py:832
  282.3 5.2 %collective-permute-done.21 = f32[2,488,128]{2,1,0:T(8,128)S(1)} collective-permute-done((f32[2,488,128]{2,1,0:T(8,128)S(1)}, f32[2,488,128]{2,1,0:T(8,128)S(1)}, u32[]{:S(2)}, u32[]{:S(2)}) %collective-permute-start.21) | collective-permute-done | bytes 499744 | tf_op jit(solution)/shard_map/ppermute | solution.py:832
  289.8 4.0 %collective-permute-done.22.refs_3_ = f32[4,976,128]{2,1,0:T(8,128)S(1)} collective-permute-done((f32[4,976,128]{2,1,0:T(8,128)S(1)}, f32[4,976,128]{2,1,0:T(8,128)S(1)}, u32[]{:S(2)}, u32[]{:S(2)}) %collective-permute-start.22) | collective-permute-done | bytes 1998880 | tf_op jit(solution)/shard_map/ppermute | solution.py:832
  293.8 3.1 %unpack.3 = (f32[2,2048,128]{2,1,0:T(8,128)}, f32[2,512,512]{2,1,0:T(8,128)}, f32[2,512,128]{2,1,0:T(8,128)}, f32[2,1536,128]{2,1,0:T(8,128)}, f32[2,2,128]{2,1,...) custom-call(s32[2]{0:T(128)S(1)} %copy-done.1, ...), custom_call_target="tpu_custom_call", output_to_operand_aliasing={{0}: (4, {}), {1}: (5, {}), {2}: (6, {})} | custom-call | flops 4600000000 | tf_op jit(solution)/shard_map/unpack/pallas_call | solution.py:42
  (77 shorter events, 34.9 us)
Async XLA Ops:
  7.2 146.0 %reduce-scatter.3.cloned.1.call-start = ((), (), s32[]{:S(2)}) async-start(), calls=%async_computation.2 | async-start | bytes 10616832 | tf_op jit(solution)/shard_map/reduce_scatter | solution.py:1036
  73.9 139.9 %reduce-scatter.5.cloned.1.call-start = ((), (), s32[]{:S(2)}) async-start(), calls=%async_computation.3 | async-start | bytes 1474560 | tf_op jit(solution)/shard_map/reduce_scatter | solution.py:1046
  130.0 12.8 %collective-permute-start = (f32[4,4,768,128]{3,2,1,0:T(8,128)}, f32[4,4,768,128]{3,2,1,0:T(8,128)}, u32[]{:S(2)}, u32[]{:S(2)}) collective-permute-start(f32[4,4,768,128]{3,2,1,0:T(8,128)} %get-tuple-element.116), channel_id=1, source_target_pairs={{0,4},{4,0},{8,12},{12,8},{16,20},{20,16},{24,28},{28,24},{1,5},{5... | collective-permute-start | bytes 18874376 | tf_op jit(solution)/shard_map/ppermute | solution.py:832
  147.8 37.7 %collective-permute-start.2 = (f32[2,2,2,384,128]{4,3,2,1,0:T(8,128)}, f32[2,2,2,384,128]{4,3,2,1,0:T(8,128)}, u32[]{:S(2)}, u32[]{:S(2)}) collective-permute-start(f32[2,2,2,384,128]{4,3,2,1,0:T(8,128)} %get-tuple-element.130), channel_id=1, source_target_pairs={{0,16},{4,20},{8,24},{12,28},{16,0},{20,4},{24,8},{28,12},{1,17},{... | collective-permute-start | bytes 4718600 | tf_op jit(solution)/shard_map/ppermute | solution.py:832
  150.2 36.8 %collective-permute-start.1 = (f32[2,2,2,384,128]{4,3,2,1,0:T(8,128)}, f32[2,2,2,384,128]{4,3,2,1,0:T(8,128)}, u32[]{:S(2)}, u32[]{:S(2)}) collective-permute-start(f32[2,2,2,384,128]{4,3,2,1,0:T(8,128)} %get-tuple-element.117.refs_0_), channel_id=1, source_target_pairs={{0,8},{4,12},{8,0},{12,4},{16,24},{20,28},{24,16},{28,20},{1,9},{5... | collective-permute-start | bytes 4718600 | tf_op jit(solution)/shard_map/ppermute | solution.py:832
  153.3 108.6 %all-gather.2.cloned.1.call-start = ((), (), s32[]{:S(2)}) async-start(), calls=%async_computation.4 | async-start | bytes 2654208 | tf_op jit(solution)/shard_map/all_gather | solution.py:1060
  176.6 16.0 %collective-permute-start.3 = (f32[4,4,208,128]{3,2,1,0:T(8,128)}, f32[4,4,208,128]{3,2,1,0:T(8,128)}, u32[]{:S(2)}, u32[]{:S(2)}) collective-permute-start(f32[4,4,208,128]{3,2,1,0:T(8,128)} %get-tuple-element.133), channel_id=1, source_target_pairs={{0,4},{4,0},{8,12},{12,8},{16,20},{20,16},{24,28},{28,24},{1,5},{5... | collective-permute-start | bytes 5111816 | tf_op jit(solution)/shard_map/ppermute | solution.py:832
  190.5 19.0 %collective-permute-start.5 = (f32[2,2,384,128]{3,2,1,0:T(8,128)}, f32[2,2,384,128]{3,2,1,0:T(8,128)S(1)}, u32[]{:S(2)}, u32[]{:S(2)}) collective-permute-start(f32[2,2,384,128]{3,2,1,0:T(8,128)} %get-tuple-element.135), channel_id=1, source_target_pairs={{0,8},{4,12},{8,0},{12,4},{16,24},{20,28},{24,16},{28,20},{1,9},{5... | collective-permute-start | bytes 2359304 | tf_op jit(solution)/shard_map/ppermute | solution.py:832
  192.1 18.9 %collective-permute-start.4 = (f32[2,2,384,128]{3,2,1,0:T(8,128)}, f32[2,2,384,128]{3,2,1,0:T(8,128)}, u32[]{:S(2)}, u32[]{:S(2)}) collective-permute-start(f32[2,2,384,128]{3,2,1,0:T(8,128)} %get-tuple-element.131.refs_0_), channel_id=1, source_target_pairs={{0,16},{4,20},{8,24},{12,28},{16,0},{20,4},{24,8},{28,12},{1,17},{... | collective-permute-start | bytes 2359304 | tf_op jit(solution)/shard_map/ppermute | solution.py:832
  209.5 1.4 copy-start.4
  213.8 10.2 %collective-permute-start.7 = (f32[2,2,2,104,128]{4,3,2,1,0:T(8,128)}, f32[2,2,2,104,128]{4,3,2,1,0:T(8,128)S(1)}, u32[]{:S(2)}, u32[]{:S(2)}) collective-permute-start(f32[2,2,2,104,128]{4,3,2,1,0:T(8,128)} %get-tuple-element.137), channel_id=1, source_target_pairs={{0,16},{4,20},{8,24},{12,28},{16,0},{20,4},{24,8},{28,12},{1,17},{... | collective-permute-start | bytes 1277960 | tf_op jit(solution)/shard_map/ppermute | solution.py:832
  214.4 11.7 %collective-permute-start.6 = (f32[2,2,2,104,128]{4,3,2,1,0:T(8,128)}, f32[2,2,2,104,128]{4,3,2,1,0:T(8,128)S(1)}, u32[]{:S(2)}, u32[]{:S(2)}) collective-permute-start(f32[2,2,2,104,128]{4,3,2,1,0:T(8,128)} %get-tuple-element.134.refs_0_), channel_id=1, source_target_pairs={{0,8},{4,12},{8,0},{12,4},{16,24},{20,28},{24,16},{28,20},{1,9},{5... | collective-permute-start | bytes 1277960 | tf_op jit(solution)/shard_map/ppermute | solution.py:832
  223.9 2.2 copy-start.7
  229.0 8.2 %collective-permute-start.9 = (f32[2,2,104,128]{3,2,1,0:T(8,128)}, f32[2,2,104,128]{3,2,1,0:T(8,128)}, u32[]{:S(2)}, u32[]{:S(2)}) collective-permute-start(f32[2,2,104,128]{3,2,1,0:T(8,128)} %get-tuple-element.139), channel_id=1, source_target_pairs={{0,8},{4,12},{8,0},{12,4},{16,24},{20,28},{24,16},{28,20},{1,9},{5... | collective-permute-start | bytes 638984 | tf_op jit(solution)/shard_map/ppermute | solution.py:832
  231.4 8.4 %collective-permute-start.8 = (f32[2,2,104,128]{3,2,1,0:T(8,128)}, f32[2,2,104,128]{3,2,1,0:T(8,128)}, u32[]{:S(2)}, u32[]{:S(2)}) collective-permute-start(f32[2,2,104,128]{3,2,1,0:T(8,128)} %get-tuple-element.138.refs_0_), channel_id=1, source_target_pairs={{0,16},{4,20},{8,24},{12,28},{16,0},{20,4},{24,8},{28,12},{1,17},{... | collective-permute-start | bytes 638984 | tf_op jit(solution)/shard_map/ppermute | solution.py:832
  232.0 18.0 %collective-permute-start.11 = (f32[2,384,128]{2,1,0:T(8,128)}, f32[2,384,128]{2,1,0:T(8,128)S(1)}, u32[]{:S(2)}, u32[]{:S(2)}) collective-permute-start(f32[2,384,128]{2,1,0:T(8,128)} %get-tuple-element.141), channel_id=1, source_target_pairs={{0,2},{1,3},{2,0},{3,1},{4,6},{5,7},{6,4},{7,5},{8,10},{9,11},{10,... | collective-permute-start | bytes 1179656 | tf_op jit(solution)/shard_map/ppermute | solution.py:832
  235.4 16.0 %collective-permute-start.10 = (f32[2,384,128]{2,1,0:T(8,128)}, f32[2,384,128]{2,1,0:T(8,128)S(1)}, u32[]{:S(2)}, u32[]{:S(2)}) collective-permute-start(f32[2,384,128]{2,1,0:T(8,128)} %get-tuple-element.136.refs_0_), channel_id=1, source_target_pairs={{0,1},{1,0},{2,3},{3,2},{4,5},{5,4},{6,7},{7,6},{8,9},{9,8},{10,11... | collective-permute-start | bytes 1179656 | tf_op jit(solution)/shard_map/ppermute | solution.py:832
  241.7 16.4 %collective-permute-start.13 = (f32[2,104,128]{2,1,0:T(8,128)}, f32[2,104,128]{2,1,0:T(8,128)S(1)}, u32[]{:S(2)}, u32[]{:S(2)}) collective-permute-start(f32[2,104,128]{2,1,0:T(8,128)} %get-tuple-element.143), channel_id=1, source_target_pairs={{0,2},{1,3},{2,0},{3,1},{4,6},{5,7},{6,4},{7,5},{8,10},{9,11},{10,... | collective-permute-start | bytes 319496 | tf_op jit(solution)/shard_map/ppermute | solution.py:832
  245.9 12.2 %collective-permute-start.12 = (f32[2,104,128]{2,1,0:T(8,128)}, f32[2,104,128]{2,1,0:T(8,128)}, u32[]{:S(2)}, u32[]{:S(2)}) collective-permute-start(f32[2,104,128]{2,1,0:T(8,128)} %get-tuple-element.140.refs_0_), channel_id=1, source_target_pairs={{0,1},{1,0},{2,3},{3,2},{4,5},{5,4},{6,7},{7,6},{8,9},{9,8},{10,11... | collective-permute-start | bytes 319496 | tf_op jit(solution)/shard_map/ppermute | solution.py:832
  250.1 1.3 copy-start.5
  254.5 12.1 %collective-permute-start.15 = (f32[384,128]{1,0:T(8,128)}, f32[384,128]{1,0:T(8,128)S(1)}, u32[]{:S(2)}, u32[]{:S(2)}) collective-permute-start(f32[384,128]{1,0:T(8,128)} %get-tuple-element.146), channel_id=1, source_target_pairs={{0,1},{1,0},{2,3},{3,2},{4,5},{5,4},{6,7},{7,6},{8,9},{9,8},{10,11... | collective-permute-start | bytes 589832 | tf_op jit(solution)/shard_map/ppermute | solution.py:832
  254.9 6.9 %copy-start.1 = (s32[2]{0:T(128)S(1)}, s32[2]{0:T(128)}, u32[]{:S(2)}) copy-start(s32[2]{0:T(128)} %pad_add_fusion.refs_1_.refs_0_) | copy-start | bytes 28
  254.9 11.7 %collective-permute-start.14 = (f32[384,128]{1,0:T(8,128)}, f32[384,128]{1,0:T(8,128)S(1)}, u32[]{:S(2)}, u32[]{:S(2)}) collective-permute-start(f32[384,128]{1,0:T(8,128)} %get-tuple-element.142.refs_0_), channel_id=1, source_target_pairs={{0,2},{1,3},{2,0},{3,1},{4,6},{5,7},{6,4},{7,5},{8,10},{9,11},{10,... | collective-permute-start | bytes 589832 | tf_op jit(solution)/shard_map/ppermute | solution.py:832
  260.4 6.2 %collective-permute-start.17 = (f32[104,128]{1,0:T(8,128)}, f32[104,128]{1,0:T(8,128)S(1)}, u32[]{:S(2)}, u32[]{:S(2)}) collective-permute-start(f32[104,128]{1,0:T(8,128)} %get-tuple-element.147), channel_id=1, source_target_pairs={{0,1},{1,0},{2,3},{3,2},{4,5},{5,4},{6,7},{7,6},{8,9},{9,8},{10,11... | collective-permute-start | bytes 159752 | tf_op jit(solution)/shard_map/ppermute | solution.py:832
  260.5 6.1 %collective-permute-start.16 = (f32[104,128]{1,0:T(8,128)}, f32[104,128]{1,0:T(8,128)S(1)}, u32[]{:S(2)}, u32[]{:S(2)}) collective-permute-start(f32[104,128]{1,0:T(8,128)} %get-tuple-element.144.refs_1_), channel_id=1, source_target_pairs={{0,2},{1,3},{2,0},{3,1},{4,6},{5,7},{6,4},{7,5},{8,10},{9,11},{10,... | collective-permute-start | bytes 159752 | tf_op jit(solution)/shard_map/ppermute | solution.py:832
  261.8 1.7 copy-start.2
  270.1 6.5 %collective-permute-start.20 = (f32[488,128]{1,0:T(8,128)}, f32[488,128]{1,0:T(8,128)S(1)}, u32[]{:S(2)}, u32[]{:S(2)}) collective-permute-start(f32[488,128]{1,0:T(8,128)} %get-tuple-element.149), channel_id=1, source_target_pairs={{0,8},{4,12},{8,0},{12,4},{16,24},{20,28},{24,16},{28,20},{1,9},{5... | collective-permute-start | bytes 749576 | tf_op jit(solution)/shard_map/ppermute | solution.py:832
  270.4 9.0 %collective-permute-start.18 = (f32[488,128]{1,0:T(8,128)}, f32[488,128]{1,0:T(8,128)S(1)}, u32[]{:S(2)}, u32[]{:S(2)}) collective-permute-start(f32[488,128]{1,0:T(8,128)} %get-tuple-element.148.refs_1_), channel_id=1, source_target_pairs={{0,16},{4,20},{8,24},{12,28},{16,0},{20,4},{24,8},{28,12},{1,17},{... | collective-permute-start | bytes 749576 | tf_op jit(solution)/shard_map/ppermute | solution.py:832
  277.6 10.0 %collective-permute-start.21 = (f32[2,488,128]{2,1,0:T(8,128)S(1)}, f32[2,488,128]{2,1,0:T(8,128)S(1)}, u32[]{:S(2)}, u32[]{:S(2)}) collective-permute-start(f32[2,488,128]{2,1,0:T(8,128)S(1)} %get-tuple-element.163), channel_id=1, source_target_pairs={{0,16},{4,20},{8,24},{12,28},{16,0},{20,4},{24,8},{28,12},{1,17},{... | collective-permute-start | bytes 1499144 | tf_op jit(solution)/shard_map/ppermute | solution.py:832
  280.4 9.0 %collective-permute-start.19 = (f32[2,488,128]{2,1,0:T(8,128)S(1)}, f32[2,488,128]{2,1,0:T(8,128)S(1)}, u32[]{:S(2)}, u32[]{:S(2)}) collective-permute-start(f32[2,488,128]{2,1,0:T(8,128)S(1)} %get-tuple-element.161), channel_id=1, source_target_pairs={{0,8},{4,12},{8,0},{12,4},{16,24},{20,28},{24,16},{28,20},{1,9},{5... | collective-permute-start | bytes 1499144 | tf_op jit(solution)/shard_map/ppermute | solution.py:832
  289.6 4.2 %copy-start = (f32[488,128]{1,0:T(8,128)S(1)}, f32[488,128]{1,0:T(8,128)}, u32[]{:S(2)}) copy-start(f32[488,128]{1,0:T(8,128)} %get-tuple-element.148.refs_1_) | copy-start | bytes 749572
  289.7 4.1 %collective-permute-start.22 = (f32[4,976,128]{2,1,0:T(8,128)S(1)}, f32[4,976,128]{2,1,0:T(8,128)S(1)}, u32[]{:S(2)}, u32[]{:S(2)}) collective-permute-start(f32[4,976,128]{2,1,0:T(8,128)S(1)} %bitcast.27), channel_id=1, source_target_pairs={{0,4},{4,0},{8,12},{12,8},{16,20},{20,16},{24,28},{28,24},{1,5},{5... | collective-permute-start | bytes 5996552 | tf_op jit(solution)/shard_map/ppermute | solution.py:832
  (8 other events, 5.7 us)
Sparse Core Ops, SparseCore 0:
  74.0 79.2 reduce-scatter.2
  155.5 29.1 reduce-scatter.4
  213.9 31.4 all-gather.1

commit v2 on v1

--- a/solution.py
+++ b/solution.py
@@ -254,8 +254,7 @@
             phi_q, phi_k = phi_q_ref[head, rows, :], phi_k_ref[head, rows, :]
             d_kernel = dot_nt(x, y).astype(BF16) * own_ref[b]
             d_phi_q[rows, :] = dot(d_kernel, phi_k)
-            d_kernel_t = dot_nt(y, x).astype(BF16) * own_t_ref[b]
-            d_phi_k[rows, :] = dot(d_kernel_t, phi_q)
+            d_phi_k[rows, :] = dot(d_kernel.T, phi_q)
             kernel_t = dot_nt(phi_k, phi_q).astype(BF16) * own_t_ref[b]
             d_v[head, rows, :] = dot(kernel_t, dn_ref[rows, :])
             if b > 0:
@@ -264,8 +263,7 @@
                 bottom = pl.ds(b * BLOCK - REACH, REACH)
                 d_kernel = dot_nt(x_ref[head, top, :], y_ref[head, earlier, :]).astype(BF16) * before_ref[b - 1]
                 d_phi_q[top, :] += dot(d_kernel, phi_k_ref[head, earlier, :])
-                d_kernel_t = dot_nt(y_ref[head, bottom, :], x).astype(BF16) * before_t_ref[b - 1]
-                d_phi_k[bottom, :] += dot(d_kernel_t, phi_q)
+                d_phi_k[bottom, :] += dot(d_kernel.T[BLOCK - REACH :, :], phi_q_ref[head, top, :])
                 kernel_t = dot_nt(phi_k_ref[head, bottom, :], phi_q).astype(BF16) * before_t_ref[b - 1]
                 d_v[head, bottom, :] += dot(kernel_t, dn_ref[rows, :])
         high, low = split_two(fm_ref[head])
@@ -289,6 +287,22 @@
         dv_ref[rows, :] = jnp.where(lane, d_v[0, rows, :], d_v[1, rows, :]).astype(BF16)
 
 
+def attn_bwd_scratch():
+    return [
+        pltpu.VMEM((BLOCKS, BLOCK, BLOCK), BF16),
+        pltpu.VMEM((BLOCKS - 1, REACH, BLOCK), BF16),
+        pltpu.VMEM((BLOCKS, BLOCK, BLOCK), BF16),
+        pltpu.VMEM((BLOCKS - 1, REACH, BLOCK), BF16),
+        pltpu.VMEM((2, LIVE, 256), BF16),
+        pltpu.VMEM((2, LIVE, 256), BF16),
+        pltpu.VMEM((LIVE, LANES), BF16),
+        pltpu.VMEM((LIVE, 256), F32),
+        pltpu.VMEM((LIVE, 256), F32),
+        pltpu.VMEM((2, LIVE, LANES), F32),
+        pltpu.VMEM((2, 2, LIVE, 256), F32),
+    ]
+
+
 def attn_bwd(layer, lengths, att_g, att, rden, phi_q, phi_k, uq, uk, v, fm, first, count, us, after=()):
     per_pair = pl.BlockSpec((1, LIVE, LANES), lambda p, *_: (first + p, 0, 0))
     per_head = pl.BlockSpec((2, LIVE, 256), lambda p, *_: (first + p, 0, 0))
@@ -301,19 +315,7 @@
         in_specs=[pl.BlockSpec((LIVE, LANES), lambda p, *_: (0, first + p)), per_pair, per_pair, per_head, per_head, per_pair, per_pair, per_pair,
                   pl.BlockSpec((None, 2) + fm.shape[2:], lambda p, *_: (layer, first + p, 0, 0))],
         out_specs=[pl.BlockSpec((LIVE, LANES), lambda p, *_: (0, p))] * 3,
-        scratch=[
-            pltpu.VMEM((BLOCKS, BLOCK, BLOCK), BF16),
-            pltpu.VMEM((BLOCKS - 1, REACH, BLOCK), BF16),
-            pltpu.VMEM((BLOCKS, BLOCK, BLOCK), BF16),
-            pltpu.VMEM((BLOCKS - 1, REACH, BLOCK), BF16),
-            pltpu.VMEM((2, LIVE, 256), BF16),
-            pltpu.VMEM((2, LIVE, 256), BF16),
-            pltpu.VMEM((LIVE, LANES), BF16),
-            pltpu.VMEM((LIVE, 256), F32),
-            pltpu.VMEM((LIVE, 256), F32),
-            pltpu.VMEM((2, LIVE, LANES), F32),
-            pltpu.VMEM((2, 2, LIVE, 256), F32),
-        ],
+        scratch=attn_bwd_scratch(),
         out_shape=[jax.ShapeDtypeStruct((LIVE, count * LANES), BF16)] * 3,
         us=us,
         name="attn_backward",
@@ -622,7 +624,7 @@
     )
 
 
-def input_bwd_body(layer, runs, parts, order, ends, id_ref, *refs):
+def input_bwd_body(layer, runs, parts, order, ends, id_ref, *refs, step=None, tiles=None):
     left_refs = refs[: 3 * runs]
     w_ref, normed_t_ref, x_ref, gain_ref, mid_g_ref = refs[3 * runs : 3 * runs + 5]
     small_refs = refs[3 * runs + 5 : -4]
@@ -630,8 +632,9 @@
         out_ref, small_ref, sent_ref, kept_ref = refs[-4:]
     else:
         out_ref, small_ref = refs[-2:]
-    step = pl.program_id(0)
-    tiles = pl.num_programs(0) - (2 if ends else 0)
+    if step is None:
+        step = pl.program_id(0)
+        tiles = pl.num_programs(0) - (2 if ends else 0)
 
     @pl.when(step == 0)
     def _():
@@ -683,6 +686,52 @@
                         for quarter in range(quarters):
                             start = quarter * per + first
                             end_ref[portion ^ ids[0], quarter ^ ids[1], base + offset : base + offset + 1, :] = source[row : row + 1, start : start + LANES]
+
+
+def attn_input_body(layer, pairs, len_ref, *refs):
+    att_refs, (w_any, x_ref, gain_ref, mid_g_ref, *outs) = refs[:9], refs[9:]
+    proj_refs, out_ref, small_ref = outs[:3], outs[3], outs[4]
+    attn_scratch, late, w_ref, sems = outs[5:16], outs[16:19], outs[19], outs[20]
+    step = pl.program_id(0)
+    fetch(step, 0, pairs, [w_any.at[layer]], [w_ref], sems)
+
+    @pl.when(step < pairs)
+    def _():
+        attn_bwd_body(len_ref, *att_refs, *proj_refs, *attn_scratch)
+        for one, whole in zip(proj_refs, late):
+            whole[:, pl.ds(pl.multiple_of(step * LANES, LANES), LANES)] = one[...]
+
+    @pl.when(step >= pairs)
+    def _():
+        tile = step - pairs
+        input_bwd_body(layer, 1, 1, (), False, None, *late, w_ref, None, x_ref, gain_ref, mid_g_ref, out_ref, small_ref, step=tile, tiles=pl.num_programs(0) - pairs)
+
+
+def attn_input_bwd(layer, lengths, att_g, att, rden, phi_q, phi_k, uq, uk, v, fm, w, x, gains, mid_g, after=()):
+    length, width = x.shape
+    tiles = length // BLOCK
+    pairs = fm.shape[1] // 2
+    pair = lambda i: jnp.minimum(i, pairs - 1)
+    per_pair = pl.BlockSpec((1, LIVE, LANES), lambda i, *_: (pair(i), 0, 0))
+    per_head = pl.BlockSpec((2, LIVE, 256), lambda i, *_: (pair(i), 0, 0))
+    column = pl.BlockSpec((LIVE, LANES), lambda i, *_: (0, pair(i)))
+    rows = pl.BlockSpec((BLOCK, width), lambda i, *_: (jnp.clip(i - pairs, 0, tiles - 1), 0))
+    return call(
+        functools.partial(attn_input_body, layer, pairs),
+        after,
+        grid=(pairs + tiles,),
+        prefetch=[lengths],
+        operands=[att_g, att, rden, phi_q, phi_k, uq, uk, v, fm, w, x, gains, mid_g],
+        in_specs=[column, per_pair, per_pair, per_head, per_head, per_pair, per_pair, per_pair]
+        + [pl.BlockSpec((None, 2) + fm.shape[2:], lambda i, *_: (layer, pair(i), 0, 0)), anywhere(), rows, constant(*gains.shape), rows],
+        out_specs=[column] * 3 + [rows, resident(8, width)],
+        scratch=attn_bwd_scratch()
+        + [pltpu.VMEM((LIVE, width), BF16)] * 3
+        + [pltpu.VMEM(w.shape[1:], w.dtype), pltpu.SemaphoreType.DMA((1,))],
+        out_shape=[jax.ShapeDtypeStruct((LIVE, width), BF16)] * 3 + [jax.ShapeDtypeStruct((length, width), F32), jax.ShapeDtypeStruct((8, width), F32)],
+        us=1.0,
+        name="attn_input_backward",
+    )
 
 
 def input_bwd(layer, ids, parts, quarters, proj_g, w, normed_t, x, gains, mid_g, smalls=(), order=(), ends=True, after=()):
@@ -1034,8 +1083,11 @@
         return (("down", layer, base, ff_rows[0]), ("up", layer, base + ff_rows[0], ff_rows[1]), ("out", layer, base + ff_rows[0] + ff_rows[1], ff_rows[2]))
 
     first = lax.psum_scatter(first.reshape(-1, LANES), "dp", scatter_dimension=0, tiled=True)
-    runs = [attn_part(1, att_g, 0, pairs, 1.0)]
-    grad, _ = input_part(1, runs, mid_g, ends=False)
+    phi_q, phi_k, uq, uk, v, att, rden = kept_one
+    *proj_g, grad, smalls[1][0] = line(
+        attn_input_bwd, 1, proteins, att_g, att, rden, phi_q, phi_k, uq, uk, v, feature_maps, qkv_weights, x_two, gains, mid_g
+    )
+    runs = [proj_g]
     mid_g, att_g, smalls[0][1], smalls[0][2], sent, kept = line(
         ff_bwd, 0, ids, parts, quarters, grad, low_t, gains, shifts, up_weights, up_bias, down_weights, out_weights, mid, (normed_one_t, runs)
     )
@@ -1057,8 +1109,8 @@
     second.step()
     third.step()
     second.step()
+    third.step()
     first = lax.all_gather(line(hold, first), "dp", tiled=True).reshape(parts, -1, LANES)
-    third.step()
     third.step()
     second.step()
     third.step()

time: 309 us -> 309 us (level)
  waiting for transfers between devices: 60.1 us -> 68 us
  starting transfers between devices: 33.5 us -> 29.3 us
  Pallas kernels: 188 us -> 184 us
    ppermute x23, starting transfers between devices: 33.3 us -> 29 us  [swap(): lax.ppermute(block, axis_name, [(i, i ^ bit) for i in range(lax.axis_size...]
    ppermute x23, waiting for transfers between devices: 58.5 us -> 62.5 us  [swap(): lax.ppermute(block, axis_name, [(i, i ^ bit) for i in range(lax.axis_size...]
    reduce_scatter x1, waiting for transfers between devices: 1.55 us -> 5.52 us  [per_device(): lax.psum_scatter(first.reshape(-1, LANES), 'dp', scatter_dimension=0, til...]
    pallas_call x21 -> x20, Pallas kernels: 188 us -> 184 us  [call(): pl.pallas_call(ordered, grid_spec=pltpu.PrefetchScalarGridSpec(num_scalar...]
  transfers between devices with their start and end apart: 26 -> 26, of which waited for: 14 -> 14; matrix products, arithmetic and copies ran while one was open for 1% -> 1% of each run, Pallas kernels for 38% -> 37%
where the time goes in v2:
time: 309 us; the launch traced here: 303 us
  Pallas kernels  184 us (60%)
  waiting for transfers between devices  68 us (22%)
  starting transfers between devices  29.3 us (9%)
  between operations  14.1 us (5%)
  local copies, waits for them, and re-layouts  4.75 us (2%)
    pallas_call x20, Pallas kernels, call(): pl.pallas_call(ordered, grid_spec=pltpu.PrefetchScalarGridSpec(num_scalar...  184 us
    ppermute x23, waiting for transfers between devices, swap(): lax.ppermute(block, axis_name, [(i, i ^ bit) for i in range(lax.axis_size...  62.5 us
    ppermute x23, starting transfers between devices, swap(): lax.ppermute(block, axis_name, [(i, i ^ bit) for i in range(lax.axis_size...  29 us
  transfers between devices with their start and end apart: 26, of which 14 were waited for; matrix products, arithmetic and copies ran while one was open for 1% of the time, Pallas kernels for 37%

profile of v2, /device:TPU:0, one launch (start us, length us, event | category | flops | bytes accessed | tf_op | source)
XLA Modules:
  0.0 303.1 jit_solution(2239664631353315751)
XLA Ops:
  7.9 25.0 %layer_forward.1 = (bf16[512,768]{1,0:T(8,128)(2,1)}, bf16[8,768,256]{2,1,0:T(8,128)(2,1)}, bf16[8,768,256]{2,1,0:T(8,128)(2,1)}, f32[4,768,128]{2,1,0:T(8,128)}...) custom-call(s32[6]{0:T(128)} %bitcast.59, ...), custom_call_target="tpu_custom_call" | custom-call | flops 23000000512 | tf_op jit(solution)/shard_map/layer_forward/pallas_call | solution.py:42
  32.8 41.0 %layer_top.1 = (bf16[512,768]{1,0:T(8,128)(2,1)}, bf16[8,768,256]{2,1,0:T(8,128)(2,1)}, bf16[8,768,256]{2,1,0:T(8,128)(2,1)}, f32[4,768,128]{2,1,0:T(8,128)}, f3...) custom-call(s32[6]{0:T(128)} %bitcast.60, ...), custom_call_target="tpu_custom_call" | custom-call | flops 23000000512 | tf_op jit(solution)/shard_map/layer_top/pallas_call | solution.py:42
  73.9 25.1 %attn_input_backward.1 = (bf16[768,512]{1,0:T(8,128)(2,1)}, bf16[768,512]{1,0:T(8,128)(2,1)}, bf16[768,512]{1,0:T(8,128)(2,1)}, f32[1024,512]{1,0:T(8,128)}, f32[8,512]{1,0:T(8,128)}) custom-call(s32[6]{0:T(128)} %bitcast.61, f32[1,2048]{1,0:T(1,128)} %get-tuple-element.87.refs_1_.refs_17_, f32[768,512]{1,0:T(8,128)} %get-tuple-element.88.refs_2_, ...), custom_call_target="tpu_custom_call" | custom-call | flops 1150000000 | tf_op jit(solution)/shard_map/attn_input_backward/pallas_call | solution.py:42
  99.0 28.0 %ff_backward.1 = (f32[1024,512]{1,0:T(8,128)}, f32[768,512]{1,0:T(8,128)}, f32[8,512]{1,0:T(8,128)}, f32[1,2048]{1,0:T(1,128)}, f32[4,4,768,128]{3,2,1,0:T(8,128)}, /*index=5*/f32[4,4,768,128]{3,2,1,0:T(8,128)}) custom-call(s32[2]{0:T(128)} %pad_add_fusion.refs_1_.refs_0_, f32[8,512]{1,0:T(8,128)} %get-tuple-element.97.refs_1_.refs_15_, ...), custom_call_target="tpu_custom_call" | custom-call | flops 20700000256 | tf_op jit(solution)/shard_map/ff_backward/pallas_call | solution.py:42
  127.5 12.3 %attn_backward.2 = (bf16[768,256]{1,0:T(8,128)(2,1)}, bf16[768,256]{1,0:T(8,128)(2,1)}, bf16[768,256]{1,0:T(8,128)(2,1)}) custom-call(s32[6]{0:T(128)} %bitcast.62, f32[1,2048]{1,0:T(1,128)} %get-tuple-element.105.refs_1_.refs_14_, f32[768,512]{1,0:T(8,128)} %get-tuple-element.106.refs_2_, f32[4,768,128]{2,1,0:T(8,128)} %get-tuple-element.107.refs_3_, ...), custom_call_target="tpu_custom_call" | custom-call | flops 69000003584 | tf_op jit(solution)/shard_map/attn_backward/pallas_call | solution.py:42
  139.8 4.9 %sums_to_send.8 = (f32[2,2,2,384,128]{4,3,2,1,0:T(8,128)}, f32[2,2,2,384,128]{4,3,2,1,0:T(8,128)}) custom-call(bf16[768,256]{1,0:T(8,128)(2,1)} %get-tuple-element.114.refs_0_.refs_2_, f32[2,2,2,2,768,128]{5,4,3,2,1,0:T(8,128)} %bitcast.31, f32[2,2,2,2,768,128]{5,4,3,2,1,0:T(8,128)} %bitcast.7.refs_2_.refs_4_.refs_5_.refs_6_.refs_7_.refs_8_, ...), custom_call_target="tpu_custom_call" | custom-call | flops 2300000000 | tf_op jit(solution)/shard_map/sums_to_send/pallas_call | solution.py:42
  144.7 3.4 %collective-permute-start.2 = (f32[2,2,2,384,128]{4,3,2,1,0:T(8,128)}, f32[2,2,2,384,128]{4,3,2,1,0:T(8,128)}, u32[]{:S(2)}, u32[]{:S(2)}) collective-permute-start(f32[2,2,2,384,128]{4,3,2,1,0:T(8,128)} %get-tuple-element.130), channel_id=1, source_target_pairs={{0,16},{4,20},{8,24},{12,28},{16,0},{20,4},{24,8},{28,12},{1,17},{... | collective-permute-start | bytes 4718600 | tf_op jit(solution)/shard_map/ppermute | solution.py:881
  149.7 5.5 %reduce-scatter.3.cloned.1.call-done.refs_1_ = f32[2304,128]{1,0:T(8,128)} async-done(((f32[18432,128]{1,0:T(8,128)}), f32[2304,128]{1,0:T(8,128)}) %reduce-scatter.3.cloned.1.call-update) | async-done | bytes 1179664 | tf_op jit(solution)/shard_map/reduce_scatter | solution.py:1085
  155.2 11.9 %attn_backward.3 = (bf16[768,256]{1,0:T(8,128)(2,1)}, bf16[768,256]{1,0:T(8,128)(2,1)}, bf16[768,256]{1,0:T(8,128)(2,1)}) custom-call(s32[6]{0:T(128)} %bitcast.63, f32[2304,128]{1,0:T(8,128)} %hold.2.refs_1_, f32[768,512]{1,0:T(8,128)} %get-tuple-element.106.refs_2_, f32[4,768,128]{2,1,0:T(8,128)} %get-tuple-element.107.refs_3_, ...), custom_call_target="tpu_custom_call" | custom-call | flops 1150000000 | tf_op jit(solution)/shard_map/attn_backward/pallas_call | solution.py:42
  167.1 11.0 %input_backward.1 = (f32[1024,512]{1,0:T(8,128)}, f32[8,512]{1,0:T(8,128)}, f32[4,4,208,128]{3,2,1,0:T(8,128)}, f32[4,4,208,128]{3,2,1,0:T(8,128)}) custom-call(s32[2]{0:T(128)} %pad_add_fusion.refs_1_.refs_0_, bf16[768,256]{1,0:T(8,128)(2,1)} %get-tuple-element.119.refs_1_.refs_5_, bf16[768,256]{1,0:T(8,128)(2,1)} %get-tuple-element.114.refs_0_.refs_2_, ...), custom_call_target="tpu_custom_call" | custom-call | flops 1150000000 | tf_op jit(solution)/shard_map/input_backward/pallas_call | solution.py:42
  178.4 6.9 %collective-permute-done.2.refs_6_.refs_7_.refs_8_.refs_9_ = f32[2,2,2,384,128]{4,3,2,1,0:T(8,128)} collective-permute-done((f32[2,2,2,384,128]{4,3,2,1,0:T(8,128)}, f32[2,2,2,384,128]{4,3,2,1,0:T(8,128)}, u32[]{:S(2)}, u32[]{:S(2)}) %collective-permute-start.2) | collective-permute-done | bytes 1572896 | tf_op jit(solution)/shard_map/ppermute | solution.py:881
  185.4 3.6 %sums_to_send.9 = (f32[2,2,384,128]{3,2,1,0:T(8,128)}, f32[2,2,384,128]{3,2,1,0:T(8,128)}) custom-call(f32[8,512]{1,0:T(8,128)} %get-tuple-element.129.refs_0_, f32[2,2,2,2,768,128]{5,4,3,2,1,0:T(8,128)} %bitcast.33, f32[2,2,2,2,768,128]{5,4,3,2,1,0:T(8,128)} %bitcast.7.refs_2_.refs_4_.refs_5_.refs_6_.refs_7_.refs_8_, ...), custom_call_target="tpu_custom_call" | custom-call | flops 2300000000 | tf_op jit(solution)/shard_map/sums_to_send/pallas_call | solution.py:42
  191.0 2.4 sums_to_send.10
  195.3 14.2 %collective-permute-done.5.refs_8_.refs_9_.refs_10_ = f32[2,2,384,128]{3,2,1,0:T(8,128)S(1)} collective-permute-done((f32[2,2,384,128]{3,2,1,0:T(8,128)}, f32[2,2,384,128]{3,2,1,0:T(8,128)S(1)}, u32[]{:S(2)}, u32[]{:S(2)}) %collective-permute-start.5) | collective-permute-done | bytes 786464 | tf_op jit(solution)/shard_map/ppermute | solution.py:881
  211.2 2.8 sums_to_send.11
  214.0 5.0 %collective-permute-done.7.refs_6_.refs_7_.refs_8_.refs_21_ = f32[2,2,2,104,128]{4,3,2,1,0:T(8,128)} collective-permute-done((f32[2,2,2,104,128]{4,3,2,1,0:T(8,128)}, f32[2,2,2,104,128]{4,3,2,1,0:T(8,128)}, u32[]{:S(2)}, u32[]{:S(2)}) %collective-permute-start.7) | collective-permute-done | bytes 426016 | tf_op jit(solution)/shard_map/ppermute | solution.py:881
  219.0 2.2 sums_to_send.12
  223.3 2.3 collective-permute-start.11
  228.0 2.0 sums_to_send.13
  230.0 2.3 collective-permute-start.13
  233.8 10.3 %collective-permute-done.11.refs_10_.refs_11_ = f32[2,384,128]{2,1,0:T(8,128)S(1)} collective-permute-done((f32[2,384,128]{2,1,0:T(8,128)}, f32[2,384,128]{2,1,0:T(8,128)S(1)}, u32[]{:S(2)}, u32[]{:S(2)}) %collective-permute-start.11) | collective-permute-done | bytes 393248 | tf_op jit(solution)/shard_map/ppermute | solution.py:881
  246.1 2.4 sums_to_send.14
  248.8 2.1 collective-permute-start.14
  251.6 1.7 sums_to_send.15
  253.4 2.4 collective-permute-start.16
  258.3 2.3 unpack.2
  260.6 1.8 collective-permute-done.16.refs_18_
  263.1 2.7 last_terms.1
  268.1 5.8 %collective-permute-done.20 = f32[488,128]{1,0:T(8,128)S(1)} collective-permute-done((f32[488,128]{1,0:T(8,128)}, f32[488,128]{1,0:T(8,128)S(1)}, u32[]{:S(2)}, u32[]{:S(2)}) %collective-permute-start.20) | collective-permute-done | bytes 249888 | tf_op jit(solution)/shard_map/ppermute | solution.py:881
  278.3 9.0 %collective-permute-done.21 = f32[2,488,128]{2,1,0:T(8,128)S(1)} collective-permute-done((f32[2,488,128]{2,1,0:T(8,128)S(1)}, f32[2,488,128]{2,1,0:T(8,128)S(1)}, u32[]{:S(2)}, u32[]{:S(2)}) %collective-permute-start.21) | collective-permute-done | bytes 499744 | tf_op jit(solution)/shard_map/ppermute | solution.py:881
  289.3 4.0 %collective-permute-done.22.refs_3_ = f32[4,976,128]{2,1,0:T(8,128)S(1)} collective-permute-done((f32[4,976,128]{2,1,0:T(8,128)S(1)}, f32[4,976,128]{2,1,0:T(8,128)S(1)}, u32[]{:S(2)}, u32[]{:S(2)}) %collective-permute-start.22) | collective-permute-done | bytes 1998880 | tf_op jit(solution)/shard_map/ppermute | solution.py:881
  293.3 3.1 %unpack.3 = (f32[2,2048,128]{2,1,0:T(8,128)}, f32[2,512,512]{2,1,0:T(8,128)}, f32[2,512,128]{2,1,0:T(8,128)}, f32[2,1536,128]{2,1,0:T(8,128)}, f32[2,2,128]{2,1,...) custom-call(s32[2]{0:T(128)S(1)} %copy-done.1, ...), custom_call_target="tpu_custom_call", output_to_operand_aliasing={{0}: (4, {}), {1}: (5, {}), {2}: (6, {})} | custom-call | flops 4600000000 | tf_op jit(solution)/shard_map/unpack/pallas_call | solution.py:42
  (72 shorter events, 29.6 us)
Async XLA Ops:
  7.2 148.0 %reduce-scatter.3.cloned.1.call-start = ((), (), s32[]{:S(2)}) async-start(), calls=%async_computation.2 | async-start | bytes 10616832 | tf_op jit(solution)/shard_map/reduce_scatter | solution.py:1085
  73.8 147.3 %reduce-scatter.5.cloned.1.call-start = ((), (), s32[]{:S(2)}) async-start(), calls=%async_computation.3 | async-start | bytes 1474560 | tf_op jit(solution)/shard_map/reduce_scatter | solution.py:1098
  127.0 12.8 %collective-permute-start = (f32[4,4,768,128]{3,2,1,0:T(8,128)}, f32[4,4,768,128]{3,2,1,0:T(8,128)}, u32[]{:S(2)}, u32[]{:S(2)}) collective-permute-start(f32[4,4,768,128]{3,2,1,0:T(8,128)} %get-tuple-element.116), channel_id=1, source_target_pairs={{0,4},{4,0},{8,12},{12,8},{16,20},{20,16},{24,28},{28,24},{1,5},{5... | collective-permute-start | bytes 18874376 | tf_op jit(solution)/shard_map/ppermute | solution.py:881
  144.7 40.6 %collective-permute-start.2 = (f32[2,2,2,384,128]{4,3,2,1,0:T(8,128)}, f32[2,2,2,384,128]{4,3,2,1,0:T(8,128)}, u32[]{:S(2)}, u32[]{:S(2)}) collective-permute-start(f32[2,2,2,384,128]{4,3,2,1,0:T(8,128)} %get-tuple-element.130), channel_id=1, source_target_pairs={{0,16},{4,20},{8,24},{12,28},{16,0},{20,4},{24,8},{28,12},{1,17},{... | collective-permute-start | bytes 4718600 | tf_op jit(solution)/shard_map/ppermute | solution.py:881
  148.1 37.2 %collective-permute-start.1 = (f32[2,2,2,384,128]{4,3,2,1,0:T(8,128)}, f32[2,2,2,384,128]{4,3,2,1,0:T(8,128)}, u32[]{:S(2)}, u32[]{:S(2)}) collective-permute-start(f32[2,2,2,384,128]{4,3,2,1,0:T(8,128)} %get-tuple-element.117.refs_0_), channel_id=1, source_target_pairs={{0,8},{4,12},{8,0},{12,4},{16,24},{20,28},{24,16},{28,20},{1,9},{5... | collective-permute-start | bytes 4718600 | tf_op jit(solution)/shard_map/ppermute | solution.py:881
  178.1 12.9 %collective-permute-start.3 = (f32[4,4,208,128]{3,2,1,0:T(8,128)}, f32[4,4,208,128]{3,2,1,0:T(8,128)}, u32[]{:S(2)}, u32[]{:S(2)}) collective-permute-start(f32[4,4,208,128]{3,2,1,0:T(8,128)} %get-tuple-element.133), channel_id=1, source_target_pairs={{0,4},{4,0},{8,12},{12,8},{16,20},{20,16},{24,28},{28,24},{1,5},{5... | collective-permute-start | bytes 5111816 | tf_op jit(solution)/shard_map/ppermute | solution.py:881
  178.2 77.6 %all-gather.2.cloned.1.call-start = ((), (), s32[]{:S(2)}) async-start(), calls=%async_computation.4 | async-start | bytes 2654208 | tf_op jit(solution)/shard_map/all_gather | solution.py:1113
  188.9 20.6 %collective-permute-start.5 = (f32[2,2,384,128]{3,2,1,0:T(8,128)}, f32[2,2,384,128]{3,2,1,0:T(8,128)S(1)}, u32[]{:S(2)}, u32[]{:S(2)}) collective-permute-start(f32[2,2,384,128]{3,2,1,0:T(8,128)} %get-tuple-element.135), channel_id=1, source_target_pairs={{0,8},{4,12},{8,0},{12,4},{16,24},{20,28},{24,16},{28,20},{1,9},{5... | collective-permute-start | bytes 2359304 | tf_op jit(solution)/shard_map/ppermute | solution.py:881
  190.4 20.8 %collective-permute-start.4 = (f32[2,2,384,128]{3,2,1,0:T(8,128)}, f32[2,2,384,128]{3,2,1,0:T(8,128)}, u32[]{:S(2)}, u32[]{:S(2)}) collective-permute-start(f32[2,2,384,128]{3,2,1,0:T(8,128)} %get-tuple-element.131.refs_0_), channel_id=1, source_target_pairs={{0,16},{4,20},{8,24},{12,28},{16,0},{20,4},{24,8},{28,12},{1,17},{... | collective-permute-start | bytes 2359304 | tf_op jit(solution)/shard_map/ppermute | solution.py:881
  193.3 25.6 %collective-permute-start.7 = (f32[2,2,2,104,128]{4,3,2,1,0:T(8,128)}, f32[2,2,2,104,128]{4,3,2,1,0:T(8,128)}, u32[]{:S(2)}, u32[]{:S(2)}) collective-permute-start(f32[2,2,2,104,128]{4,3,2,1,0:T(8,128)} %get-tuple-element.137), channel_id=1, source_target_pairs={{0,16},{4,20},{8,24},{12,28},{16,0},{20,4},{24,8},{28,12},{1,17},{... | collective-permute-start | bytes 1277960 | tf_op jit(solution)/shard_map/ppermute | solution.py:881
  194.8 24.2 %collective-permute-start.6 = (f32[2,2,2,104,128]{4,3,2,1,0:T(8,128)}, f32[2,2,2,104,128]{4,3,2,1,0:T(8,128)}, u32[]{:S(2)}, u32[]{:S(2)}) collective-permute-start(f32[2,2,2,104,128]{4,3,2,1,0:T(8,128)} %get-tuple-element.134.refs_0_), channel_id=1, source_target_pairs={{0,8},{4,12},{8,0},{12,4},{16,24},{20,28},{24,16},{28,20},{1,9},{5... | collective-permute-start | bytes 1277960 | tf_op jit(solution)/shard_map/ppermute | solution.py:881
  209.6 1.6 copy-start.4
  221.2 6.3 %collective-permute-start.9 = (f32[2,2,104,128]{3,2,1,0:T(8,128)}, f32[2,2,104,128]{3,2,1,0:T(8,128)}, u32[]{:S(2)}, u32[]{:S(2)}) collective-permute-start(f32[2,2,104,128]{3,2,1,0:T(8,128)} %get-tuple-element.139), channel_id=1, source_target_pairs={{0,8},{4,12},{8,0},{12,4},{16,24},{20,28},{24,16},{28,20},{1,9},{5... | collective-permute-start | bytes 638984 | tf_op jit(solution)/shard_map/ppermute | solution.py:881
  221.9 6.2 %collective-permute-start.8 = (f32[2,2,104,128]{3,2,1,0:T(8,128)}, f32[2,2,104,128]{3,2,1,0:T(8,128)}, u32[]{:S(2)}, u32[]{:S(2)}) collective-permute-start(f32[2,2,104,128]{3,2,1,0:T(8,128)} %get-tuple-element.138.refs_0_), channel_id=1, source_target_pairs={{0,16},{4,20},{8,24},{12,28},{16,0},{20,4},{24,8},{28,12},{1,17},{... | collective-permute-start | bytes 638984 | tf_op jit(solution)/shard_map/ppermute | solution.py:881
  223.3 20.9 %collective-permute-start.11 = (f32[2,384,128]{2,1,0:T(8,128)}, f32[2,384,128]{2,1,0:T(8,128)S(1)}, u32[]{:S(2)}, u32[]{:S(2)}) collective-permute-start(f32[2,384,128]{2,1,0:T(8,128)} %get-tuple-element.141), channel_id=1, source_target_pairs={{0,2},{1,3},{2,0},{3,1},{4,6},{5,7},{6,4},{7,5},{8,10},{9,11},{10,... | collective-permute-start | bytes 1179656 | tf_op jit(solution)/shard_map/ppermute | solution.py:881
  225.6 19.8 %collective-permute-start.10 = (f32[2,384,128]{2,1,0:T(8,128)}, f32[2,384,128]{2,1,0:T(8,128)S(1)}, u32[]{:S(2)}, u32[]{:S(2)}) collective-permute-start(f32[2,384,128]{2,1,0:T(8,128)} %get-tuple-element.136.refs_0_), channel_id=1, source_target_pairs={{0,1},{1,0},{2,3},{3,2},{4,5},{5,4},{6,7},{7,6},{8,9},{9,8},{10,11... | collective-permute-start | bytes 1179656 | tf_op jit(solution)/shard_map/ppermute | solution.py:881
  230.0 20.9 %collective-permute-start.13 = (f32[2,104,128]{2,1,0:T(8,128)}, f32[2,104,128]{2,1,0:T(8,128)S(1)}, u32[]{:S(2)}, u32[]{:S(2)}) collective-permute-start(f32[2,104,128]{2,1,0:T(8,128)} %get-tuple-element.143), channel_id=1, source_target_pairs={{0,2},{1,3},{2,0},{3,1},{4,6},{5,7},{6,4},{7,5},{8,10},{9,11},{10,... | collective-permute-start | bytes 319496 | tf_op jit(solution)/shard_map/ppermute | solution.py:881
  232.3 18.6 %collective-permute-start.12 = (f32[2,104,128]{2,1,0:T(8,128)}, f32[2,104,128]{2,1,0:T(8,128)}, u32[]{:S(2)}, u32[]{:S(2)}) collective-permute-start(f32[2,104,128]{2,1,0:T(8,128)} %get-tuple-element.140.refs_0_), channel_id=1, source_target_pairs={{0,1},{1,0},{2,3},{3,2},{4,5},{5,4},{6,7},{7,6},{8,9},{9,8},{10,11... | collective-permute-start | bytes 319496 | tf_op jit(solution)/shard_map/ppermute | solution.py:881
  244.2 1.2 copy-start.5
  248.5 13.9 %collective-permute-start.15 = (f32[384,128]{1,0:T(8,128)}, f32[384,128]{1,0:T(8,128)S(1)}, u32[]{:S(2)}, u32[]{:S(2)}) collective-permute-start(f32[384,128]{1,0:T(8,128)} %get-tuple-element.146), channel_id=1, source_target_pairs={{0,1},{1,0},{2,3},{3,2},{4,5},{5,4},{6,7},{7,6},{8,9},{9,8},{10,11... | collective-permute-start | bytes 589832 | tf_op jit(solution)/shard_map/ppermute | solution.py:881
  248.8 7.0 %copy-start.1 = (s32[2]{0:T(128)S(1)}, s32[2]{0:T(128)}, u32[]{:S(2)}) copy-start(s32[2]{0:T(128)} %pad_add_fusion.refs_1_.refs_0_) | copy-start | bytes 28
  248.8 13.6 %collective-permute-start.14 = (f32[384,128]{1,0:T(8,128)}, f32[384,128]{1,0:T(8,128)S(1)}, u32[]{:S(2)}, u32[]{:S(2)}) collective-permute-start(f32[384,128]{1,0:T(8,128)} %get-tuple-element.142.refs_0_), channel_id=1, source_target_pairs={{0,2},{1,3},{2,0},{3,1},{4,6},{5,7},{6,4},{7,5},{8,10},{9,11},{10,... | collective-permute-start | bytes 589832 | tf_op jit(solution)/shard_map/ppermute | solution.py:881
  253.3 7.3 %collective-permute-start.17 = (f32[104,128]{1,0:T(8,128)}, f32[104,128]{1,0:T(8,128)S(1)}, u32[]{:S(2)}, u32[]{:S(2)}) collective-permute-start(f32[104,128]{1,0:T(8,128)} %get-tuple-element.147), channel_id=1, source_target_pairs={{0,1},{1,0},{2,3},{3,2},{4,5},{5,4},{6,7},{7,6},{8,9},{9,8},{10,11... | collective-permute-start | bytes 159752 | tf_op jit(solution)/shard_map/ppermute | solution.py:881
  253.4 9.0 %collective-permute-start.16 = (f32[104,128]{1,0:T(8,128)}, f32[104,128]{1,0:T(8,128)S(1)}, u32[]{:S(2)}, u32[]{:S(2)}) collective-permute-start(f32[104,128]{1,0:T(8,128)} %get-tuple-element.144.refs_1_), channel_id=1, source_target_pairs={{0,2},{1,3},{2,0},{3,1},{4,6},{5,7},{6,4},{7,5},{8,10},{9,11},{10,... | collective-permute-start | bytes 159752 | tf_op jit(solution)/shard_map/ppermute | solution.py:881
  255.8 1.7 copy-start.2
  260.6 1.8 copy-start.10
  265.8 8.1 %collective-permute-start.20 = (f32[488,128]{1,0:T(8,128)}, f32[488,128]{1,0:T(8,128)S(1)}, u32[]{:S(2)}, u32[]{:S(2)}) collective-permute-start(f32[488,128]{1,0:T(8,128)} %get-tuple-element.149), channel_id=1, source_target_pairs={{0,8},{4,12},{8,0},{12,4},{16,24},{20,28},{24,16},{28,20},{1,9},{5... | collective-permute-start | bytes 749576 | tf_op jit(solution)/shard_map/ppermute | solution.py:881
  266.5 9.3 %collective-permute-start.18 = (f32[488,128]{1,0:T(8,128)}, f32[488,128]{1,0:T(8,128)S(1)}, u32[]{:S(2)}, u32[]{:S(2)}) collective-permute-start(f32[488,128]{1,0:T(8,128)} %get-tuple-element.148.refs_1_), channel_id=1, source_target_pairs={{0,16},{4,20},{8,24},{12,28},{16,0},{20,4},{24,8},{28,12},{1,17},{... | collective-permute-start | bytes 749576 | tf_op jit(solution)/shard_map/ppermute | solution.py:881
  274.9 12.4 %collective-permute-start.21 = (f32[2,488,128]{2,1,0:T(8,128)S(1)}, f32[2,488,128]{2,1,0:T(8,128)S(1)}, u32[]{:S(2)}, u32[]{:S(2)}) collective-permute-start(f32[2,488,128]{2,1,0:T(8,128)S(1)} %get-tuple-element.163), channel_id=1, source_target_pairs={{0,16},{4,20},{8,24},{12,28},{16,0},{20,4},{24,8},{28,12},{1,17},{... | collective-permute-start | bytes 1499144 | tf_op jit(solution)/shard_map/ppermute | solution.py:881
  276.8 12.1 %collective-permute-start.19 = (f32[2,488,128]{2,1,0:T(8,128)S(1)}, f32[2,488,128]{2,1,0:T(8,128)S(1)}, u32[]{:S(2)}, u32[]{:S(2)}) collective-permute-start(f32[2,488,128]{2,1,0:T(8,128)S(1)} %get-tuple-element.161), channel_id=1, source_target_pairs={{0,8},{4,12},{8,0},{12,4},{16,24},{20,28},{24,16},{28,20},{1,9},{5... | collective-permute-start | bytes 1499144 | tf_op jit(solution)/shard_map/ppermute | solution.py:881
  289.1 4.2 %copy-start = (f32[488,128]{1,0:T(8,128)S(1)}, f32[488,128]{1,0:T(8,128)}, u32[]{:S(2)}) copy-start(f32[488,128]{1,0:T(8,128)} %get-tuple-element.148.refs_1_) | copy-start | bytes 749572
  289.2 4.1 %collective-permute-start.22 = (f32[4,976,128]{2,1,0:T(8,128)S(1)}, f32[4,976,128]{2,1,0:T(8,128)S(1)}, u32[]{:S(2)}, u32[]{:S(2)}) collective-permute-start(f32[4,976,128]{2,1,0:T(8,128)S(1)} %bitcast.27), channel_id=1, source_target_pairs={{0,4},{4,0},{8,12},{12,8},{16,20},{20,16},{24,28},{28,24},{1,5},{5... | collective-permute-start | bytes 5996552 | tf_op jit(solution)/shard_map/ppermute | solution.py:881
  (6 other events, 4.3 us)
Sparse Core Ops, SparseCore 0:
  74.0 81.1 reduce-scatter.2
  178.3 28.6 reduce-scatter.4
  221.3 28.9 all-gather.1
